TPU v7x, 32 devices: a whole 2x2x4 slice. The times are simulated.
32 devices in a mesh: groups: 2 (over x), lon: 16 (over z, y, core).
Axes of the slice: x: 2, y: 2, z: 4, core: 2. Of those that a mesh axis runs over, the one named last changes fastest.
Arguments:
- fields: bfloat16 [32, 32, 1500], P(('groups', 'lon')), parts along dimension 0, may hold values from -6 to 6
- level_ids: int32 [6], P('groups'), parts along dimension 0, may hold values from 0 to 2, each once
- embed_weight: bfloat16 [500, 512], replicated, may hold values from -0.25 to 0.25
- level_embed: bfloat16 [3, 512], replicated, may hold values from -6 to 6
- enc_gain: float32 [512], replicated, may hold values from 0.1 to 1.9
- latent_query: bfloat16 [2, 512], replicated, may hold values from -0.049804688 to 0.049804688
- kv_weight: bfloat16 [512, 1024], replicated, may hold values from -0.25 to 0.25
- pool_out: bfloat16 [512, 512], replicated, may hold values from -0.25 to 0.25
- attn_gain: float32 [512], replicated, may hold values from 0.1 to 1.9
- qkv_weight: bfloat16 [512, 1536], replicated, may hold values from -0.25 to 0.25
- attn_proj: bfloat16 [512, 512], replicated, may hold values from -0.25 to 0.25
- mlp_gain: float32 [512], replicated, may hold values from 0.1 to 1.9
- mlp_up: bfloat16 [512, 2048], replicated, may hold values from -0.25 to 0.25
- mlp_down: bfloat16 [2048, 512], replicated, may hold values from -0.125 to 0.125
- level_mix: float32 [3, 2], replicated, may hold values from 0.25 to 4
- dec_gain: float32 [512], replicated, may hold values from 0.1 to 1.9
- dec_weight: bfloat16 [512, 500], replicated, may hold values from -0.25 to 0.25
Outputs:
- forecast: bfloat16 [32, 32, 1500], P(('groups', 'lon')), parts along dimension 0
There are 2 independent parts, one for each index of `groups`. A program takes and returns all parts, laid end to end along the dimension named above; an argument that names none is the same for every part. Nothing has to cross between parts.
Inputs may be any that keep to these rules, and one draw needn't show every extreme that they name: level_ids holds each of 0 to 2 once.
All inputs are finite; a program needn't handle non-finite values.
Results may differ from a plain program's by a relative error of at most 0.014.
Values may be sent and summed in bfloat16 or wider, within the bound.
No kernel may reach another device: no remote copies, remote signals or barrier semaphores. Data moves between devices by JAX's collectives and lax.ppermute only.
A program may use at most 128 MiB of HBM per device.

v0:
```python
import jax
import jax.numpy as jnp
from jax import lax
from jax.sharding import PartitionSpec as P

D = 512
HEADS = 8
PIN = 500
LEV = 3
LATL = 2
W_LAT = 4
W_LON = 8
STEPS = 2
ROW_PARTS = 4


norm_eps = 1e-05
head_eps = 1e-06


def product(einsum_form, left_side, right_side):
    return jnp.einsum(einsum_form, left_side, right_side, preferred_element_type=jnp.float32)


def layer_norm(values, scale_row):
    average = jnp.mean(values, axis=-1, keepdims=True)
    centred = values - average
    spread = jnp.mean(centred * centred, axis=-1, keepdims=True)
    return centred * lax.rsqrt(spread + norm_eps) * scale_row


def unit_heads(values):
    shaped = values.reshape(values.shape[:-1] + (HEADS, D // HEADS))
    mean_square = jnp.mean(shaped * shaped, axis=-1, keepdims=True)
    return (shaped * lax.rsqrt(mean_square + head_eps)).reshape(values.shape)


def level_tables(level_ids, level_embed, level_mix):
    picker = (level_ids[:, None] == jnp.arange(LEV, dtype=jnp.int32)[None, :]).astype(jnp.float32)
    embeds = jnp.dot(picker, level_embed.astype(jnp.float32), precision=lax.Precision.HIGHEST)
    mixing = jnp.dot(picker, level_mix, precision=lax.Precision.HIGHEST)
    return (embeds, mixing)


def head_tables(queries):
    head_dim = D // HEADS
    feature_head = jnp.arange(D, dtype=jnp.int32) // head_dim
    head_ids = jnp.arange(HEADS, dtype=jnp.int32)
    spreader = (head_ids[:, None] == feature_head[None, :]).astype(jnp.bfloat16)
    on_head = (feature_head[:, None] == head_ids[None, :]).astype(jnp.bfloat16)
    query_table = (queries.T[:, :, None] * on_head[:, None, :]).reshape(D, LATL * HEADS)
    return (query_table, spreader)


def encode(
    flat_fields,
    embeds,
    query_table,
    spreader,
    embed_weight,
    enc_gain,
    kv_weight,
    pool_out,
    latent_query,
):
    head_dim = D // HEADS
    patch_count = flat_fields.shape[0]
    patches = flat_fields.reshape(patch_count * LEV, PIN)
    tokens = jnp.dot(patches, embed_weight, preferred_element_type=jnp.float32).reshape(
        patch_count, LEV, D
    )
    tokens = layer_norm(tokens + embeds[None], enc_gain).astype(jnp.bfloat16)
    keyval = jnp.dot(
        tokens.reshape(patch_count * LEV, D), kv_weight, preferred_element_type=jnp.float32
    )
    key_rows = unit_heads(keyval[:, :D]).astype(jnp.bfloat16)
    value_rows = keyval[:, D:].astype(jnp.bfloat16).reshape(patch_count, LEV, 1, D)
    scores = jnp.dot(key_rows, query_table, preferred_element_type=jnp.float32) * head_dim ** (-0.5)
    scores = scores.reshape(patch_count, LEV, LATL * HEADS)
    weights = jnp.exp(scores)
    weights = (weights / jnp.sum(weights, axis=1, keepdims=True)).astype(jnp.bfloat16)
    spread_weights = jnp.dot(
        weights.reshape(patch_count * LEV * LATL, HEADS),
        spreader,
        preferred_element_type=jnp.float32,
    )
    spread_weights = spread_weights.reshape(patch_count, LEV, LATL, D)
    pooled = jnp.sum(spread_weights * value_rows.astype(jnp.float32), axis=1)
    pooled = pooled.astype(jnp.bfloat16).reshape(patch_count * LATL, D)
    latents = jnp.dot(pooled, pool_out, preferred_element_type=jnp.float32).reshape(
        patch_count, LATL, D
    )
    return (latents + latent_query.astype(jnp.float32)[None]).astype(jnp.bfloat16)


def increments(backbone_out, embeds, mixing, dec_gain, dec_weight):
    patch_count = backbone_out.shape[0]
    blended = mixing[None, :, 0, None] * backbone_out[:, None, 0, :].astype(jnp.float32)
    blended = blended + mixing[None, :, 1, None] * backbone_out[:, None, 1, :].astype(jnp.float32)
    blended = blended + embeds[None]
    normed = layer_norm(blended, dec_gain).astype(jnp.bfloat16)
    result = jnp.dot(
        normed.reshape(patch_count * LEV, D), dec_weight, preferred_element_type=jnp.float32
    )
    return result.astype(jnp.bfloat16).reshape(patch_count, LEV * PIN)


def window_block(shifted, attn_gain, qkv_weight, attn_proj):
    head_dim = D // HEADS
    lat_count, lon_count = (shifted.shape[0], shifted.shape[1])
    lat_win, lon_win = (lat_count // W_LAT, lon_count // W_LON)
    inside = W_LAT * W_LON * LATL
    flat_tokens = shifted.reshape(-1, D)
    normed = layer_norm(flat_tokens.astype(jnp.float32), attn_gain).astype(jnp.bfloat16)
    projected = jnp.dot(normed, qkv_weight, preferred_element_type=jnp.float32)
    query_heads = unit_heads(projected[:, :D]).astype(jnp.bfloat16)
    key_heads = unit_heads(projected[:, D : 2 * D]).astype(jnp.bfloat16)
    value_heads = projected[:, 2 * D :].astype(jnp.bfloat16)

    def to_windows(head_data):
        shaped = head_data.reshape(lat_win, W_LAT, lon_win, W_LON, LATL, HEADS, head_dim)
        return shaped.transpose(0, 2, 5, 1, 3, 4, 6).reshape(
            lat_win, lon_win, HEADS, inside, head_dim
        )

    scores = product(
        "abhqc,abhkc->abhqk", to_windows(query_heads), to_windows(key_heads)
    ) * head_dim ** (-0.5)
    row_index = jnp.arange(lat_count, dtype=jnp.int32).reshape(lat_win, W_LAT)
    region = (row_index >= lat_count - W_LAT // 2).astype(jnp.int32)
    region_tok = jnp.broadcast_to(region[:, :, None, None], (lat_win, W_LAT, W_LON, LATL)).reshape(
        lat_win, inside
    )
    allowed = (region_tok[:, :, None] == region_tok[:, None, :]).astype(jnp.float32)
    weights = jnp.exp(scores) * allowed[:, None, None, :, :]
    weights = (weights / jnp.sum(weights, axis=-1, keepdims=True)).astype(jnp.bfloat16)
    win_mix = product("abhqk,abhkc->abhqc", weights, to_windows(value_heads)).astype(jnp.bfloat16)
    win_mix = win_mix.reshape(lat_win, lon_win, HEADS, W_LAT, W_LON, LATL, head_dim)
    win_mix = win_mix.transpose(0, 3, 1, 4, 5, 2, 6).reshape(-1, D)
    attended = flat_tokens.astype(jnp.float32) + jnp.dot(
        win_mix, attn_proj, preferred_element_type=jnp.float32
    )
    return attended.astype(jnp.bfloat16).reshape(shifted.shape)


def mlp_block(restored, mlp_gain, mlp_up, mlp_down):
    flat_tokens = restored.reshape(-1, D)
    normed = layer_norm(flat_tokens.astype(jnp.float32), mlp_gain).astype(jnp.bfloat16)
    hidden = jax.nn.gelu(jnp.dot(normed, mlp_up, preferred_element_type=jnp.float32)).astype(
        jnp.bfloat16
    )
    result = flat_tokens.astype(jnp.float32) + jnp.dot(
        hidden, mlp_down, preferred_element_type=jnp.float32
    )
    return result.astype(jnp.bfloat16).reshape(restored.shape)


def shards(
    fields,
    level_ids,
    embed_weight,
    level_embed,
    enc_gain,
    latent_query,
    kv_weight,
    pool_out,
    attn_gain,
    qkv_weight,
    attn_proj,
    mlp_gain,
    mlp_up,
    mlp_down,
    level_mix,
    dec_gain,
    dec_weight,
):
    embeds, mixing = level_tables(level_ids, level_embed, level_mix)
    queries = unit_heads(latent_query.astype(jnp.float32)).astype(jnp.bfloat16)
    query_table, spreader = head_tables(queries)
    field_width = fields.shape[2]
    local_count = fields.shape[1]
    devices = lax.axis_size("lon")
    piece_cols = local_count // devices
    lat_count = devices // ROW_PARTS
    lon_dev = piece_cols * ROW_PARTS
    half_cols = W_LON // 2
    lag = half_cols // piece_cols
    piece = lax.axis_index("lon") // lat_count
    carry = (piece - lag) // ROW_PARTS
    latent_width = LATL * D
    current = fields
    for turn_index in range(STEPS):
        latents = encode(
            current.reshape(local_count, field_width),
            embeds,
            query_table,
            spreader,
            embed_weight,
            enc_gain,
            kv_weight,
            pool_out,
            latent_query,
        )
        blocks = latents.reshape(devices, piece_cols, latent_width)
        blocks = jnp.roll(blocks, carry, axis=0)
        got = lax.all_to_all(
            blocks.reshape(1, local_count, latent_width),
            "lon",
            split_axis=1,
            concat_axis=0,
            tiled=True,
        )
        tiles = got.reshape(ROW_PARTS, lat_count, piece_cols, latent_width).transpose(1, 0, 2, 3)
        tiles = jnp.roll(tiles, -lag, axis=1).reshape(lat_count, lon_dev, latent_width)
        tiles = jnp.roll(tiles, -(W_LAT // 2), axis=0).reshape(lat_count, lon_dev, LATL, D)
        attended = window_block(tiles, attn_gain, qkv_weight, attn_proj)
        backbone_out = mlp_block(attended, mlp_gain, mlp_up, mlp_down)
        values = backbone_out.reshape(lat_count, lon_dev, latent_width)
        extent = values.shape[2]
        values = jnp.roll(values, W_LAT // 2, axis=0)
        values = jnp.roll(values.reshape(lat_count, ROW_PARTS, piece_cols, extent), lag, axis=1)
        outgoing = values.transpose(1, 0, 2, 3).reshape(devices, piece_cols, extent)
        received = lax.all_to_all(outgoing, "lon", split_axis=0, concat_axis=1, tiled=True)
        home = received.reshape(devices, piece_cols, received.shape[2])
        home = jnp.roll(home, -carry, axis=0)
        home_latents = home.reshape(local_count, received.shape[2])
        added = increments(
            home_latents.reshape(local_count, LATL, D), embeds, mixing, dec_gain, dec_weight
        )
        added = added.reshape(current.shape)
        current = (current.astype(jnp.float32) + added.astype(jnp.float32)).astype(jnp.bfloat16)
    return current


def solution(mesh):
    placed = (
        P(("groups", "lon"), None, None),
        P("groups"),
        P(),
        P(),
        P(),
        P(),
        P(),
        P(),
        P(),
        P(),
        P(),
        P(),
        P(),
        P(),
        P(),
        P(),
        P(),
    )
    return jax.shard_map(
        shards,
        mesh=mesh,
        in_specs=placed,
        out_specs=P(("groups", "lon"), None, None),
        check_vma=False,
    )
```

profile of v0, /device:TPU:0, one launch (start us, length us, event | category | flops | bytes accessed | tf_op | source)
XLA Modules:
  0.0 169.1 jit_solution(9471271311963540494)
XLA Ops:
  7.6 1.8 %copy.290 = f32[96,512]{0,1:T(8,128)} copy(f32[96,512]{1,0:T(8,128)} %slice_multiply_fusion.1) | data formatting | bytes 393216 | tf_op jit(solution)/shard_map/mul | solution.py:34
  11.0 1.8 %copy.291 = f32[96,512]{1,0:T(8,128)} copy(f32[96,512]{0,1:T(8,128)} %bitcast.127) | data formatting | bytes 393216 | tf_op jit(solution)/shard_map/mul | solution.py:35
  21.5 1.7 fusion.17
  36.7 7.4 %all-to-all-start = ((bf16[16,2,1024]{2,1,0:T(2,128)(2,1)}), bf16[16,2,1024]{2,1,0:T(2,128)(2,1)}, u32[]{:S(2)}, u32[]{:S(2)}) async-start(bf16[16,2,1024]{2,1,0:T(2,128)(2,1)} %reshape.632), calls=%async_computation | async-start | bytes 131072 | tf_op jit(solution)/shard_map/all_to_all | solution.py:206
  47.0 4.1 %all-to-all-done = bf16[16,2,1024]{2,1,0:T(2,128)(2,1)} async-done(((bf16[16,2,1024]{2,1,0:T(2,128)(2,1)}), bf16[16,2,1024]{2,1,0:T(2,128)(2,1)}, u32[]{:S(2)}, u32[]{:S(2)}) %all-to-all-start) | async-done | bytes 65568 | tf_op jit(solution)/shard_map/all_to_all | solution.py:206
  56.0 1.9 %fusion.72 = f32[64,1536]{1,0:T(8,128)S(1)} fusion(bf16[512,1536]{1,0:T(8,128)(2,1)} %param.28, f32[64,512]{1,0:T(8,128)S(1)} %reshape.616, f32[512]{0:T(512)} %param.27, f32[64]{0:T(128)S(1)} %add_rsqrt_fusion.14, f32[64]{0:T(128)S(1)} %broadcast_multiply_fusion.7), kind=kOutput, calls=%fused_computation.140 | convolution fusion | flops 100794368 | bytes 2099712 | tf_op jit(solution)/shard_map/dot_general | solution.py:115
  59.4 1.7 %mul.492 = f32[64,8,64]{2,1,0:T(8,128)} reshape(f32[64,512]{1,0:T(8,128)} %get-tuple-element.13) | data formatting | bytes 262144 | tf_op jit(solution)/shard_map/mul | solution.py:34
  65.7 1.7 %mul.494 = f32[64,512]{1,0:T(8,128)} reshape(f32[64,8,64]{2,1,0:T(8,128)} %mul.493) | data formatting | bytes 262144 | tf_op jit(solution)/shard_map/mul | solution.py:35
  67.4 1.7 %mul.497 = f32[64,8,64]{2,1,0:T(8,128)} reshape(f32[64,512]{1,0:T(8,128)} %get-tuple-element.12) | data formatting | bytes 262144 | tf_op jit(solution)/shard_map/mul | solution.py:34
  73.7 1.7 %mul.499 = f32[64,512]{1,0:T(8,128)} reshape(f32[64,8,64]{2,1,0:T(8,128)} %mul.498) | data formatting | bytes 262144 | tf_op jit(solution)/shard_map/mul | solution.py:35
  75.4 1.8 %multiply_convert_fusion.11 = (bf16[64,512]{1,0:T(8,128)(2,1)}, bf16[64,512]{1,0:T(8,128)(2,1)}) fusion(f32[64,512]{1,0:T(8,128)} %mul.499, f32[64,1536]{1,0:T(8,128)} %copy-done.2, f32[64,512]{1,0:T(8,128)} %mul.494), kind=kLoop, calls=%fused_computation.112 | loop fusion | flops 131072 | bytes 655360 | tf_op jit(solution)/shard_map/convert_element_type | solution.py:117
  87.0 1.9 %fusion.5 = f32[8,64,64]{1,2,0:T(8,128)} fusion(bf16[8,64,64]{2,1,0:T(8,128)(2,1)} %bitcast.136, bf16[8,64,64]{2,1,0:T(8,128)(2,1)} %bitcast.138, f32[64,64]{0,1:T(8,128)S(1)} %compare_convert_fusion), kind=kOutput, calls=%fused_computation.9 | convolution fusion | flops 4259840 | bytes 278528 | tf_op jit(solution)/shard_map/abhqc,abhkc->abhqk/dot_general | solution.py:22
  88.9 2.0 %convolution_convert_fusion.1 = bf16[8,64,64]{2,1,0:T(8,128)(2,1)} fusion(bf16[8,64,64]{2,1,0:T(8,128)(2,1)} %bitcast.153, f32[8,64,64]{1,2,0:T(8,128)} %fusion.5), kind=kOutput, calls=%fused_computation.13 | convolution fusion | flops 4293183 | bytes 262144 | tf_op jit(solution)/shard_map/abhqk,abhkc->abhqc/dot_general | solution.py:22
  90.9 1.7 %copy.396 = bf16[1,1,8,4,8,2,64]{6,2,5,4,3,1,0:T(8,128)(2,1)} copy(bf16[1,1,8,4,8,2,64]{6,5,4,3,2,1,0:T(2,128)(2,1)} %bitcast.154) | data formatting | bytes 131072 | tf_op jit(solution)/shard_map/reshape | solution.py:138
  95.9 2.6 %fusion.11 = bf16[64,512]{1,0:T(8,128)(2,1)S(1)} fusion(f32[64,512]{1,0:T(8,128)} %copy-done.8, bf16[2048,512]{1,0:T(8,128)(2,1)S(1)} %copy-done, bf16[512,2048]{1,0:T(8,128)(2,1)} %param.31, f32[512]{0:T(512)} %param.30, f32[64]{0:T(128)S(1)} %add_rsqrt_fusion.13, f32[64]{0:T(128)S(1)} %broadcast_multiply_fusion.6), kind=kOutput, calls=%fused_computation.27 | convolution fusion | flops 269811712 | bytes 4393472 | tf_op jit(solution)/shard_map/dot_general | solution.py:152
  99.5 3.5 %all-to-all-start.1 = ((bf16[16,2,1024]{2,1,0:T(2,128)(2,1)}), bf16[16,2,1024]{2,1,0:T(2,128)(2,1)S(1)}, u32[]{:S(2)}, u32[]{:S(2)}) async-start(bf16[16,2,1024]{2,1,0:T(2,128)(2,1)} %bitcast.22), calls=%async_computation.1 | async-start | bytes 131072 | tf_op jit(solution)/shard_map/all_to_all | solution.py:223
  104.3 5.5 %all-to-all-done.1 = bf16[16,2,1024]{2,1,0:T(2,128)(2,1)S(1)} async-done(((bf16[16,2,1024]{2,1,0:T(2,128)(2,1)}), bf16[16,2,1024]{2,1,0:T(2,128)(2,1)S(1)}, u32[]{:S(2)}, u32[]{:S(2)}) %all-to-all-start.1) | async-done | bytes 65568 | tf_op jit(solution)/shard_map/all_to_all | solution.py:223
  113.1 1.7 %mul.516 = f32[96,512]{1,0:T(8,128)} reshape(f32[32,3,512]{2,1,0:T(4,128)} %mul.515.clone) | data formatting | bytes 393216 | tf_op jit(solution)/shard_map/mul | solution.py:98
  115.5 1.7 %mul.525 = f32[96,512]{1,0:T(8,128)} reshape(f32[32,3,512]{2,1,0:T(4,128)} %mul.524.clone) | data formatting | bytes 393216 | tf_op jit(solution)/shard_map/mul | solution.py:99
  117.3 2.2 %fusion.6 = f32[96,500]{1,0:T(8,128)} fusion(bf16[512,500]{0,1:T(8,128)(2,1)} %param.35, f32[96,512]{1,0:T(8,128)S(1)} %add.248, f32[96,512]{1,0:T(8,128)} %mul.525, f32[96,512]{1,0:T(8,128)} %mul.516, f32[512]{0:T(512)} %param.34, f32[96]{0:T(128)S(1)} %rsqrt.134, f32[96]{0:T(128)S(1)} %div.166, f32[96]{0:T(128)} %mul.520, f32[96]{0:T(128)} %mul.462), kind=kOutput, calls=%fused_computation.16 | convolution fusion | flops 49641216 | bytes 1297408 | tf_op jit(solution)/shard_map/dot_general | solution.py:102
  131.9 9.7 %all_to_all.16 = bf16[16,2,1024]{2,1,0:T(2,128)(2,1)S(1)} all-to-all(bf16[16,2,1024]{2,1,0:T(2,128)(2,1)S(1)} %reshape.634), channel_id=1, replica_groups=mesh['groups'=2,'lon'=16] {'lon'}, dimensions={0} | all-to-all | bytes 131072 | tf_op jit(solution)/shard_map/all_to_all | solution.py:206
  142.6 1.8 %fusion.74 = f32[64,1536]{1,0:T(8,128)S(1)} fusion(bf16[512,1536]{1,0:T(8,128)(2,1)} %param.28, f32[64,512]{1,0:T(8,128)S(1)} %reshape.621, f32[64]{0:T(128)S(1)} %add_rsqrt_fusion.12, f32[64]{0:T(128)S(1)} %broadcast_multiply_fusion.5, f32[512]{0:T(512)S(1)} %copy-done.20), kind=kOutput, calls=%fused_computation.142 | convolution fusion | flops 100794368 | bytes 2099712 | tf_op jit(solution)/shard_map/dot_general | solution.py:115
  152.5 2.5 %fusion.15 = bf16[64,512]{1,0:T(8,128)(2,1)S(1)} fusion(f32[64,512]{1,0:T(8,128)S(1)} %get-tuple-element.43, bf16[2048,512]{1,0:T(8,128)(2,1)S(1)} %copy-done, bf16[512,2048]{1,0:T(8,128)(2,1)} %param.31, f32[64]{0:T(128)S(1)} %add_rsqrt_fusion.11, f32[64]{0:T(128)S(1)} %broadcast_multiply_fusion.4, f32[512]{0:T(512)S(1)} %copy-done.21), kind=kOutput, calls=%fused_computation.31 | convolution fusion | flops 269811712 | bytes 4393472 | tf_op jit(solution)/shard_map/dot_general | solution.py:152
  155.4 9.5 %all_to_all.17 = bf16[16,2,1024]{2,1,0:T(2,128)(2,1)S(1)} all-to-all(bf16[16,2,1024]{2,1,0:T(2,128)(2,1)S(1)} %bitcast.151), channel_id=1, replica_groups=mesh['groups'=2,'lon'=16] {'lon'}, dimensions={0} | all-to-all | bytes 131072 | tf_op jit(solution)/shard_map/all_to_all | solution.py:223
  (281 shorter events, 94.3 us)
Async XLA Ops:
  0.0 95.8 %copy-start = (bf16[2048,512]{1,0:T(8,128)(2,1)S(1)}, bf16[2048,512]{1,0:T(8,128)(2,1)}, u32[]{:S(2)}) copy-start(bf16[2048,512]{1,0:T(8,128)(2,1)} %param.32) | copy-start | bytes 6291460
  0.0 5.7 %copy-start.1 = (bf16[512,1024]{1,0:T(8,128)(2,1)S(1)}, bf16[512,1024]{1,0:T(8,128)(2,1)}, u32[]{:S(2)}) copy-start(bf16[512,1024]{1,0:T(8,128)(2,1)} %param.25) | copy-start | bytes 3145732
  28.2 18.0 %copy-start.26 = (f32[3,2]{0,1:T(2,128)S(1)}, f32[3,2]{0,1:T(2,128)}, u32[]{:S(2)}) copy-start(f32[3,2]{0,1:T(2,128)} %param.33) | copy-start | bytes 76
  28.2 18.0 %copy-start.27 = (s32[3]{0:T(128)S(1)}, s32[3]{0:T(128)}, u32[]{:S(2)}) copy-start(s32[3]{0:T(128)} %param.20) | copy-start | bytes 40
  28.9 15.5 %copy-start.13 = (f32[2,512]{1,0:T(2,128)}, f32[2,512]{1,0:T(2,128)S(1)}, u32[]{:S(2)}) copy-start(f32[2,512]{1,0:T(2,128)S(1)} %convert_element_type.247) | copy-start | bytes 12292
  36.7 14.4 %all-to-all-start = ((bf16[16,2,1024]{2,1,0:T(2,128)(2,1)}), bf16[16,2,1024]{2,1,0:T(2,128)(2,1)}, u32[]{:S(2)}, u32[]{:S(2)}) async-start(bf16[16,2,1024]{2,1,0:T(2,128)(2,1)} %reshape.632), calls=%async_computation | async-start | bytes 131072 | tf_op jit(solution)/shard_map/all_to_all | solution.py:206
  44.4 42.6 %copy-start.11 = (f32[64,64]{0,1:T(8,128)}, f32[64,64]{0,1:T(8,128)S(1)}, u32[]{:S(2)}) copy-start(f32[64,64]{0,1:T(8,128)S(1)} %compare_convert_fusion) | copy-start | bytes 49156
  46.3 71.0 %copy-start.6 = (f32[96,512]{1,0:T(8,128)}, f32[96,512]{1,0:T(8,128)S(1)}, u32[]{:S(2)}) copy-start(f32[96,512]{1,0:T(8,128)S(1)} %add.248) | copy-start | bytes 589828
  95.8 7.1 %copy-start.25 = (f32[3,2]{0,1:T(2,128)S(1)}, f32[3,2]{0,1:T(2,128)}, u32[]{:S(2)}) copy-start(f32[3,2]{0,1:T(2,128)} %fusion.118) | copy-start | bytes 76
  99.5 10.4 %all-to-all-start.1 = ((bf16[16,2,1024]{2,1,0:T(2,128)(2,1)}), bf16[16,2,1024]{2,1,0:T(2,128)(2,1)S(1)}, u32[]{:S(2)}, u32[]{:S(2)}) async-start(bf16[16,2,1024]{2,1,0:T(2,128)(2,1)} %bitcast.22), calls=%async_computation.1 | async-start | bytes 131072 | tf_op jit(solution)/shard_map/all_to_all | solution.py:223
  103.0 6.8 %copy-start.14 = (f32[3]{0:T(128)}, f32[3]{0:T(128)S(1)}, u32[]{:S(2)}) copy-start(f32[3]{0:T(128)S(1)} %get-tuple-element.34) | copy-start | bytes 40
  103.0 6.8 %copy-start.16 = (f32[3]{0:T(128)}, f32[3]{0:T(128)S(1)}, u32[]{:S(2)}) copy-start(f32[3]{0:T(128)S(1)} %get-tuple-element.35) | copy-start | bytes 40
  114.8 8.4 %copy-start.19 = (f32[512]{0:T(512)S(1)}, f32[512]{0:T(512)}, u32[]{:S(2)}) copy-start(f32[512]{0:T(512)} %param.23) | copy-start | bytes 6148
  127.8 14.9 %copy-start.20 = (f32[512]{0:T(512)S(1)}, f32[512]{0:T(512)}, u32[]{:S(2)}) copy-start(f32[512]{0:T(512)} %param.27) | copy-start | bytes 6148
  145.6 4.7 %copy-start.12 = (f32[64,64]{0,1:T(8,128)S(1)}, f32[64,64]{0,1:T(8,128)}, u32[]{:S(2)}) copy-start(f32[64,64]{0,1:T(8,128)} %copy-done.11) | copy-start | bytes 49156
  146.5 5.4 %copy-start.4 = (bf16[512,512]{1,0:T(8,128)(2,1)S(1)}, bf16[512,512]{1,0:T(8,128)(2,1)}, u32[]{:S(2)}) copy-start(bf16[512,512]{1,0:T(8,128)(2,1)} %param.29) | copy-start | bytes 1572868
  148.1 4.3 %copy-start.21 = (f32[512]{0:T(512)S(1)}, f32[512]{0:T(512)}, u32[]{:S(2)}) copy-start(f32[512]{0:T(512)} %param.30) | copy-start | bytes 6148
  152.5 12.8 %copy-start.15 = (f32[3]{0:T(128)S(1)}, f32[3]{0:T(128)}, u32[]{:S(2)}) copy-start(f32[3]{0:T(128)} %copy-done.14) | copy-start | bytes 40
  152.5 12.8 %copy-start.17 = (f32[3]{0:T(128)S(1)}, f32[3]{0:T(128)}, u32[]{:S(2)}) copy-start(f32[3]{0:T(128)} %copy-done.16) | copy-start | bytes 40
  155.0 12.1 %copy-start.5 = (bf16[512,500]{0,1:T(8,128)(2,1)S(1)}, bf16[512,500]{0,1:T(8,128)(2,1)}, u32[]{:S(2)}) copy-start(bf16[512,500]{0,1:T(8,128)(2,1)} %param.35) | copy-start | bytes 1536004
  155.0 12.1 %copy-start.7 = (f32[96,512]{1,0:T(8,128)S(1)}, f32[96,512]{1,0:T(8,128)}, u32[]{:S(2)}) copy-start(f32[96,512]{1,0:T(8,128)} %copy-done.6) | copy-start | bytes 589828
  155.0 12.1 %copy-start.22 = (f32[512]{0:T(512)S(1)}, f32[512]{0:T(512)}, u32[]{:S(2)}) copy-start(f32[512]{0:T(512)} %param.34) | copy-start | bytes 6148
  155.0 12.1 %copy-start.23 = (f32[96]{0:T(128)S(1)}, f32[96]{0:T(128)}, u32[]{:S(2)}) copy-start(f32[96]{0:T(128)} %mul.462) | copy-start | bytes 1156
  155.1 12.0 %copy-start.24 = (f32[96]{0:T(128)S(1)}, f32[96]{0:T(128)}, u32[]{:S(2)}) copy-start(f32[96]{0:T(128)} %mul.520) | copy-start | bytes 1156
  (6 other events, 11.6 us)
where the time goes:
time: 172 us; the launch traced here: 169 us
  local copies, waits for them, and re-layouts  66.6 us (39%)
  matrix products  32.2 us (19%)
  other arithmetic  29.3 us (17%)
  blocking collectives  19.1 us (11%)
  starting transfers between devices  10.9 us (6%)
  waiting for transfers between devices  9.6 us (6%)
    mul x14, local copies, waits for them, and re-layouts, unit_heads(): return (shaped * lax.rsqrt(mean_square + head_eps)).reshape(values.shape)  10.2 us
    all_to_all x1, blocking collectives, shards(): lax.all_to_all(blocks.reshape(1, local_count, latent_width), 'lon', split...  9.66 us
    all_to_all x1, blocking collectives, shards(): lax.all_to_all(outgoing, 'lon', split_axis=0, concat_axis=1, tiled=True)  9.48 us
    all_to_all x1, starting transfers between devices, shards(): lax.all_to_all(blocks.reshape(1, local_count, latent_width), 'lon', split...  7.44 us
    reshape x6, local copies, waits for them, and re-layouts, to_windows(): head_data.reshape(lat_win, W_LAT, lon_win, W_LON, LATL, HEADS, head_dim)  6.95 us
    mul x7, local copies, waits for them, and re-layouts, unit_heads(): mean_square = jnp.mean(shaped * shaped, axis=-1, keepdims=True)  6.84 us
    transpose x6, local copies, waits for them, and re-layouts, to_windows(): shaped.transpose(0, 2, 5, 1, 3, 4, 6)  5.92 us
    all_to_all x1, waiting for transfers between devices, shards(): lax.all_to_all(outgoing, 'lon', split_axis=0, concat_axis=1, tiled=True)  5.53 us
  transfers between devices with their start and end apart: 2, of which 2 were waited for; matrix products, arithmetic and copies ran while one was open for 2% of the time, Pallas kernels for 0%

commit v1 on v0

v1 whole, which is shorter than its diff:
```python
import functools

import jax
import jax.numpy as jnp
from jax import lax
from jax.experimental import pallas as pl
from jax.experimental.pallas import tpu as pltpu
from jax.sharding import PartitionSpec as P

D = 512
HEADS = 8
HEAD_DIM = D // HEADS
PIN = 500
LEV = 3
LATL = 2
W_LAT = 4
W_LON = 8
STEPS = 2
ROW_PARTS = 4
MLP = 2048
PATCHES = W_LAT * W_LON
TOKENS = PATCHES * LATL
HALF = D // 2
PAIR = 2 * HEAD_DIM

norm_eps = 1e-05
head_eps = 1e-06

F32 = jnp.float32
BF16 = jnp.bfloat16


def mm(a, b):
    return jnp.dot(a, b, preferred_element_type=F32)


def mm_t(a, b):
    return lax.dot_general(a, b, (((1,), (1,)), ((), ())), preferred_element_type=F32)


def layer_norm(values, gain):
    average = jnp.mean(values, axis=-1, keepdims=True)
    centred = values - average
    spread = jnp.mean(centred * centred, axis=-1, keepdims=True)
    return centred * lax.rsqrt(spread + norm_eps) * gain


def iota(shape, dim):
    return lax.broadcasted_iota(jnp.int32, shape, dim)


def picked(index, rows):
    result = rows[LEV - 1]
    for i in reversed(range(LEV - 1)):
        result = jnp.where(index == i, rows[i], result)
    return result


def forecast_kernel(
    windows,
    ids_ref,
    mix_ref,
    x_ref,
    level_embed_ref,
    enc_gain_ref,
    latent_query_ref,
    attn_gain_ref,
    mlp_gain_ref,
    dec_gain_ref,
    embed_ref,
    kv_ref,
    pool_ref,
    qkv_ref,
    proj_ref,
    up_ref,
    down_ref,
    dec_ref,
    out_ref,
    state,
    wide,
):
    table = level_embed_ref[...].astype(F32)
    rows = [table[i : i + 1] for i in range(LEV)]
    embeds = [picked(ids_ref[l], rows) for l in range(LEV)]
    mixing = [[mix_ref[ids_ref[l], j] for j in range(LATL)] for l in range(LEV)]
    latent = latent_query_ref[...].astype(F32)

    row16 = iota((LATL * HEADS, D), 0)
    lane_head = iota((LATL * HEADS, D), 1) // HEAD_DIM
    on_head = (row16 % HEADS) == lane_head
    square = (latent * latent)
    query_rows = []
    for j in range(LATL):
        masked = jnp.where(on_head[:HEADS], square[j : j + 1], 0.0)
        scale = lax.rsqrt(jnp.sum(masked, axis=-1, keepdims=True) / HEAD_DIM + head_eps)
        query_rows.append(jnp.where(on_head[:HEADS], latent[j : j + 1] * scale, 0.0))
    query_table = jnp.concatenate(query_rows, axis=0).astype(BF16)
    mean_table = jnp.where(on_head, 1.0 / HEAD_DIM, 0.0).astype(BF16)
    spread_row = iota((LATL * HEADS, LATL * D), 0)
    spread_lane = iota((LATL * HEADS, LATL * D), 1)
    spreader = jnp.where(spread_row == spread_lane // HEAD_DIM, 1.0, 0.0).astype(BF16)
    block_ones = jnp.where(
        iota((HALF, HALF), 0) // HEAD_DIM == iota((HALF, HALF), 1) // HEAD_DIM, 1.0 / HEAD_DIM, 0.0
    ).astype(BF16)
    low = iota((1, PAIR), 1) < HEAD_DIM
    half_ones = jnp.where(
        (iota((PAIR, PAIR), 0) < HEAD_DIM) == (iota((PAIR, PAIR), 1) < HEAD_DIM), 1.0, 0.0
    ).astype(BF16)
    row_bit = (iota((TOKENS, PAIR), 0) // 4) % 2
    lane_bit = (iota((TOKENS, PAIR), 1) // 4) % 2
    cut = jnp.where(pl.program_id(0) == windows - 1, 1, 0)
    allowed = jnp.where((row_bit - lane_bit) * cut == 0, 1.0, 0.0)

    arrived = x_ref[0].astype(F32).reshape(PATCHES, LEV * PIN)
    for l in range(LEV):
        state[l * PATCHES : (l + 1) * PATCHES, :] = arrived[:, l * PIN : (l + 1) * PIN]

    def step(_, carry):
        patches = state[...].astype(BF16)
        tokens = mm(patches, embed_ref[...])
        tokens = jnp.concatenate(
            [tokens[l * PATCHES : (l + 1) * PATCHES] + embeds[l] for l in range(LEV)], axis=0
        )
        tokens = layer_norm(tokens, enc_gain_ref[...]).astype(BF16)
        keyval = mm(tokens, kv_ref[...])
        keys = keyval[:, :D]
        values = keyval[:, D:].astype(BF16).astype(F32)
        mean_square = mm_t((keys * keys).astype(BF16), mean_table)
        scores = mm_t(keys.astype(BF16), query_table)
        scores = scores * lax.rsqrt(mean_square + head_eps) * HEAD_DIM ** (-0.5)
        weights = jnp.exp(scores)
        parts = [weights[l * PATCHES : (l + 1) * PATCHES] for l in range(LEV)]
        inverse = 1.0 / (parts[0] + parts[1] + parts[2])
        weights = jnp.concatenate([part * inverse for part in parts], axis=0).astype(BF16)
        wide_weights = mm(weights, spreader)
        pooled = []
        for j in range(LATL):
            total = None
            for l in range(LEV):
                term = (
                    wide_weights[l * PATCHES : (l + 1) * PATCHES, j * D : (j + 1) * D]
                    * values[l * PATCHES : (l + 1) * PATCHES]
                )
                total = term if total is None else total + term
            pooled.append(total)
        pooled = jnp.concatenate(pooled, axis=0).astype(BF16)
        latents = mm(pooled, pool_ref[...])
        latents = jnp.concatenate(
            [latents[j * PATCHES : (j + 1) * PATCHES] + latent[j : j + 1] for j in range(LATL)],
            axis=0,
        )
        normed = layer_norm(latents, attn_gain_ref[...]).astype(BF16)
        projected = mm(normed, qkv_ref[...])
        halves = jnp.concatenate(
            [projected[:, i * HALF : (i + 1) * HALF] for i in range(4)], axis=0
        )
        mean_square = mm((halves * halves).astype(BF16), block_ones)
        halves = halves * lax.rsqrt(mean_square + head_eps)
        win_values = projected[:, 2 * D :]
        mixed = []
        for pair in range(HEADS // 2):
            half, at = pair // 2, (pair % 2) * PAIR
            query = halves[half * TOKENS : (half + 1) * TOKENS, at : at + PAIR].astype(BF16)
            key = halves[(2 + half) * TOKENS : (3 + half) * TOKENS, at : at + PAIR]
            value = win_values[:, pair * PAIR : (pair + 1) * PAIR]
            key = jnp.concatenate(
                [jnp.where(low, key, 0.0), jnp.where(low, 0.0, key)], axis=0
            ).astype(BF16)
            value = jnp.concatenate(
                [jnp.where(low, value, 0.0), jnp.where(low, 0.0, value)], axis=0
            ).astype(BF16)
            weights = jnp.exp(mm_t(query, key) * HEAD_DIM ** (-0.5)) * allowed
            weights = weights.astype(BF16)
            both = mm(weights, jnp.concatenate([value, half_ones], axis=1))
            mixed.append((both[:, :PAIR] / both[:, PAIR:]).astype(BF16))
        attended = latents + mm(jnp.concatenate(mixed, axis=1), proj_ref[...])
        normed = layer_norm(attended, mlp_gain_ref[...]).astype(BF16)
        hidden = jax.nn.gelu(mm(normed, up_ref[...])).astype(BF16)
        backbone = attended + mm(hidden, down_ref[...])
        blended = jnp.concatenate(
            [
                mixing[l][0] * backbone[:PATCHES] + mixing[l][1] * backbone[PATCHES:] + embeds[l]
                for l in range(LEV)
            ],
            axis=0,
        )
        normed = layer_norm(blended, dec_gain_ref[...]).astype(BF16)
        state[...] = (state[...] + mm(normed, dec_ref[...])).astype(BF16).astype(F32)
        return carry

    lax.fori_loop(0, STEPS, step, 0)
    for l in range(LEV):
        wide[:, l * PIN : (l + 1) * PIN] = state[l * PATCHES : (l + 1) * PATCHES, :]
    out_ref[0] = wide[...].reshape(PATCHES // 2, 2, LEV * PIN).astype(BF16)


def turn_kernel(step, direction, x_ref, out_ref):
    count = x_ref.shape[0] if len(x_ref.shape) == 3 else out_ref.shape[0]
    turned = lax.axis_index("lon") < step
    blocks = x_ref[...].astype(F32).reshape(count, 2, LEV * PIN)

    @pl.when(turned)
    def _():
        if direction > 0:
            moved = jnp.concatenate([blocks[1:], blocks[:1]], axis=0)
        else:
            moved = jnp.concatenate([blocks[-1:], blocks[:-1]], axis=0)
        out_ref[...] = moved.reshape(out_ref.shape).astype(BF16)

    @pl.when(jnp.logical_not(turned))
    def _():
        out_ref[...] = blocks.reshape(out_ref.shape).astype(BF16)


def turn(array, shape, step, direction):
    return pl.pallas_call(
        functools.partial(turn_kernel, step, direction),
        out_shape=jax.ShapeDtypeStruct(shape, BF16),
    )(array)


def forecast(windows, arranged, ids, mix, *tensors):
    vmem = pl.BlockSpec(memory_space=pltpu.VMEM)
    smem = pl.BlockSpec(memory_space=pltpu.SMEM)
    block = pl.BlockSpec((1,) + arranged.shape[1:], lambda i: (i, 0, 0, 0))
    return pl.pallas_call(
        functools.partial(forecast_kernel, windows),
        grid=(windows,),
        in_specs=[smem, smem, block] + [vmem] * len(tensors),
        out_specs=block,
        out_shape=jax.ShapeDtypeStruct(arranged.shape, BF16),
        scratch_shapes=[
            pltpu.VMEM((LEV * PATCHES, PIN), F32),
            pltpu.VMEM((PATCHES, LEV * PIN), F32),
        ],
        compiler_params=pltpu.CompilerParams(vmem_limit_bytes=40 * 1024 * 1024),
    )(ids, mix, arranged, *tensors)


def shards(
    fields,
    level_ids,
    embed_weight,
    level_embed,
    enc_gain,
    latent_query,
    kv_weight,
    pool_out,
    attn_gain,
    qkv_weight,
    attn_proj,
    mlp_gain,
    mlp_up,
    mlp_down,
    level_mix,
    dec_gain,
    dec_weight,
):
    devices = lax.axis_size("lon")
    width = fields.shape[2]
    local_count = fields.shape[1]
    piece_cols = local_count // devices
    lat_count = devices // ROW_PARTS
    bands = lat_count // W_LAT
    cut = (W_LON // 2 // piece_cols) * lat_count
    outgoing = turn(fields.reshape(local_count, width), (devices, piece_cols, width), cut, 1)
    got = lax.all_to_all(outgoing, "lon", split_axis=0, concat_axis=0, tiled=True)
    if bands > 1:
        got = got.reshape(ROW_PARTS, lat_count, piece_cols, width)
        got = jnp.roll(got, -(W_LAT // 2), axis=1)
        got = got.reshape(ROW_PARTS, bands, W_LAT, piece_cols, width).transpose(1, 0, 2, 3, 4)
    arranged = got.reshape(bands, ROW_PARTS * W_LAT, piece_cols, width)
    done = forecast(
        bands,
        arranged,
        level_ids,
        level_mix,
        level_embed,
        enc_gain.reshape(1, D),
        latent_query,
        attn_gain.reshape(1, D),
        mlp_gain.reshape(1, D),
        dec_gain.reshape(1, D),
        embed_weight,
        kv_weight,
        pool_out,
        qkv_weight,
        attn_proj,
        mlp_up,
        mlp_down,
        dec_weight,
    )
    if bands > 1:
        done = done.reshape(bands, ROW_PARTS, W_LAT, piece_cols, width).transpose(1, 0, 2, 3, 4)
        done = done.reshape(ROW_PARTS, lat_count, piece_cols, width)
        done = jnp.roll(done, W_LAT // 2, axis=1)
    done = done.reshape(devices, piece_cols, width)
    home = lax.all_to_all(done, "lon", split_axis=0, concat_axis=0, tiled=True)
    return turn(home, (local_count, width), cut, -1).reshape(fields.shape)


def solution(mesh):
    placed = (P(("groups", "lon"), None, None), P("groups")) + (P(),) * 15
    return jax.shard_map(
        shards,
        mesh=mesh,
        in_specs=placed,
        out_specs=P(("groups", "lon"), None, None),
        check_vma=False,
    )
```

time: 172 us -> 50.5 us (0.29); the launches traced: 169 us -> 49.8 us
  local copies, waits for them, and re-layouts: 66.6 us -> 14.5 us
  matrix products: 32.2 us -> 0 us
  other arithmetic: 29.3 us -> 0 us
  Pallas kernels: 0 us -> 11.8 us
  blocking collectives: 19.1 us -> 10.7 us
  waiting for transfers between devices: 9.6 us -> 5.39 us
  starting transfers between devices: 10.9 us -> 7.39 us
    dot_general x24 -> x0, matrix products: 32.2 us -> none  [the longest x4 5.2 us: product(): jnp.einsum(einsum_form, left_side, right_side, preferred_element_type=jnp...]
    mul x34 -> x0, local copies, waits for them, and re-layouts: 24.2 us -> none  [the longest x14 10.2 us: unit_heads(): return (shaped * lax.rsqrt(mean_square + head_eps)).reshape(values.shape)]
    reshape x18 -> x0, local copies, waits for them, and re-layouts: 12.6 us -> none  [the longest x6 6.95 us: to_windows(): head_data.reshape(lat_win, W_LAT, lon_win, W_LON, LATL, HEADS, head_dim)]
    pallas_call x0 -> x3, Pallas kernels: none -> 11.8 us  [the longest x1 8.52 us: forecast(): pl.pallas_call(functools.partial(forecast_kernel, windows), grid=(windows...]
    unnamed x66 -> x30, local copies, waits for them, and re-layouts: 3.62 us -> 14.5 us
    convert_element_type x16 -> x0, other arithmetic: 9.59 us -> none  [the longest x2 2.44 us: window_block(): key_heads = unit_heads(projected[:, D:2 * D]).astype(jnp.bfloat16)]
    reduce_sum x21 -> x0, other arithmetic: 9.14 us -> none  [the longest x7 4.84 us: unit_heads(): mean_square = jnp.mean(shaped * shaped, axis=-1, keepdims=True)]
    all_to_all x2 -> x1, blocking collectives: 19.1 us -> 10.7 us  [shards(): home = lax.all_to_all(done, 'lon', split_axis=0, concat_axis=0, tiled=True)]
  transfers between devices with their start and end apart: 2 -> 1, of which waited for: 2 -> 1; matrix products, arithmetic and copies ran while one was open for 2% -> 4% of each run, Pallas kernels for 0% -> 0%
where the time goes in v1:
time: 50.5 us; the launch traced here: 49.8 us
  local copies, waits for them, and re-layouts  14.5 us (29%)
  Pallas kernels  11.8 us (23%)
  blocking collectives  10.7 us (21%)
  starting transfers between devices  7.39 us (15%)
  waiting for transfers between devices  5.39 us (11%)
    unnamed x30, local copies, waits for them, and re-layouts  14.5 us
    all_to_all x1, blocking collectives, shards(): home = lax.all_to_all(done, 'lon', split_axis=0, concat_axis=0, tiled=True)  10.7 us
    pallas_call x1, Pallas kernels, forecast(): pl.pallas_call(functools.partial(forecast_kernel, windows), grid=(windows...  8.52 us
    all_to_all x1, starting transfers between devices, shards(): lax.all_to_all(outgoing, 'lon', split_axis=0, concat_axis=0, tiled=True)  7.39 us
    all_to_all x1, waiting for transfers between devices, shards(): lax.all_to_all(outgoing, 'lon', split_axis=0, concat_axis=0, tiled=True)  5.39 us
    pallas_call x2, Pallas kernels, turn(): pl.pallas_call(functools.partial(turn_kernel, step, direction), out_shape...  3.3 us
  transfers between devices with their start and end apart: 1, of which 1 were waited for; matrix products, arithmetic and copies ran while one was open for 4% of the time, Pallas kernels for 0%

profile of v1, /device:TPU:0, one launch (start us, length us, event | category | flops | bytes accessed | tf_op | source)
XLA Modules:
  0.0 49.8 jit_solution(16482652292918857617)
XLA Ops:
  0.0 0.0 copy-start.3
  0.0 1.7 %shard_map.163 = bf16[16,2,1500]{2,1,0:T(2,128)(2,1)} custom-call(bf16[32,1500]{1,0:T(8,128)(2,1)} %bitcast.14), custom_call_target="tpu_custom_call" | custom-call | tf_op jit(solution)/shard_map/pallas_call | solution.py:216
  1.7 7.4 %all-to-all-start = ((bf16[16,2,1500]{2,1,0:T(2,128)(2,1)}), bf16[16,2,1500]{2,1,0:T(2,128)(2,1)S(1)}, u32[]{:S(2)}, u32[]{:S(2)}) async-start(bf16[16,2,1500]{2,1,0:T(2,128)(2,1)} %shard_map.163), calls=%async_computation | async-start | bytes 196608 | tf_op jit(solution)/shard_map/all_to_all | solution.py:267
  9.1 0.8 %copy.18.mix_ref = f32[3,2]{1,0:T(4,128)S(1)} copy(f32[3,2]{0,1:T(2,128)} %param.31) | data formatting | bytes 48 | tf_op args[14]
  9.9 1.2 %copy.19.dec_ref = bf16[512,500]{1,0:T(8,128)(2,1)S(1)} copy(bf16[512,500]{0,1:T(8,128)(2,1)} %param.33) | data formatting | bytes 1024000 | tf_op args[16]
  11.1 5.4 %all-to-all-done = bf16[16,2,1500]{2,1,0:T(2,128)(2,1)S(1)} async-done(((bf16[16,2,1500]{2,1,0:T(2,128)(2,1)}), bf16[16,2,1500]{2,1,0:T(2,128)(2,1)S(1)}, u32[]{:S(2)}, u32[]{:S(2)}) %all-to-all-start) | async-done | bytes 96032 | tf_op jit(solution)/shard_map/all_to_all | solution.py:267
  16.5 0.0 copy-done.3
  16.5 0.0 copy-start
  16.5 1.6 %copy-done = bf16[512,2048]{1,0:T(8,128)(2,1)S(1)} copy-done((bf16[512,2048]{1,0:T(8,128)(2,1)S(1)}, bf16[512,2048]{1,0:T(8,128)(2,1)}, u32[]{:S(2)}) %copy-start) | copy-done | bytes 2097176
  18.1 1.6 %copy-done.1 = bf16[2048,512]{1,0:T(8,128)(2,1)S(1)} copy-done((bf16[2048,512]{1,0:T(8,128)(2,1)S(1)}, bf16[2048,512]{1,0:T(8,128)(2,1)}, u32[]{:S(2)}) %copy-start.1) | copy-done | bytes 2097176
  19.7 1.4 %copy-done.2 = bf16[512,1536]{1,0:T(8,128)(2,1)S(1)} copy-done((bf16[512,1536]{1,0:T(8,128)(2,1)S(1)}, bf16[512,1536]{1,0:T(8,128)(2,1)}, u32[]{:S(2)}) %copy-start.2) | copy-done | bytes 1572888
  21.1 1.0 %copy-done.4 = bf16[512,512]{1,0:T(8,128)(2,1)S(1)} copy-done((bf16[512,512]{1,0:T(8,128)(2,1)S(1)}, bf16[512,512]{1,0:T(8,128)(2,1)}, u32[]{:S(2)}) %copy-start.4) | copy-done | bytes 524312
  22.2 1.0 %copy-done.5 = bf16[512,512]{1,0:T(8,128)(2,1)S(1)} copy-done((bf16[512,512]{1,0:T(8,128)(2,1)S(1)}, bf16[512,512]{1,0:T(8,128)(2,1)}, u32[]{:S(2)}) %copy-start.5) | copy-done | bytes 524312
  23.2 1.0 %copy-done.6 = bf16[500,512]{1,0:T(8,128)(2,1)S(1)} copy-done((bf16[500,512]{1,0:T(8,128)(2,1)S(1)}, bf16[500,512]{1,0:T(8,128)(2,1)}, u32[]{:S(2)}) %copy-start.6) | copy-done | bytes 512024
  24.3 0.7 %copy-done.7 = bf16[3,512]{1,0:T(4,128)(2,1)S(1)} copy-done((bf16[3,512]{1,0:T(4,128)(2,1)S(1)}, bf16[3,512]{1,0:T(4,128)(2,1)}, u32[]{:S(2)}) %copy-start.7) | copy-done | bytes 3096
  24.9 0.7 %copy-done.8 = f32[512]{0:T(512)S(1)} copy-done((f32[512]{0:T(512)S(1)}, f32[512]{0:T(512)}, u32[]{:S(2)}) %copy-start.8) | copy-done | bytes 2072
  25.6 0.7 %copy-done.9 = bf16[2,512]{1,0:T(2,128)(2,1)S(1)} copy-done((bf16[2,512]{1,0:T(2,128)(2,1)S(1)}, bf16[2,512]{1,0:T(2,128)(2,1)}, u32[]{:S(2)}) %copy-start.9) | copy-done | bytes 2072
  26.3 0.7 %copy-done.10 = f32[512]{0:T(512)S(1)} copy-done((f32[512]{0:T(512)S(1)}, f32[512]{0:T(512)}, u32[]{:S(2)}) %copy-start.10) | copy-done | bytes 2072
  27.0 0.7 %copy-done.11 = f32[512]{0:T(512)S(1)} copy-done((f32[512]{0:T(512)S(1)}, f32[512]{0:T(512)}, u32[]{:S(2)}) %copy-start.11) | copy-done | bytes 2072
  27.7 0.7 %copy-done.12 = f32[512]{0:T(512)S(1)} copy-done((f32[512]{0:T(512)S(1)}, f32[512]{0:T(512)}, u32[]{:S(2)}) %copy-start.12) | copy-done | bytes 2072
  28.4 0.7 %copy-done.13 = s32[3]{0:T(128)S(1)} copy-done((s32[3]{0:T(128)S(1)}, s32[3]{0:T(128)}, u32[]{:S(2)}) %copy-start.13) | copy-done | bytes 36
  29.0 8.5 %shard_map.164 = bf16[1,16,2,1500]{3,2,1,0:T(2,128)(2,1)S(1)} custom-call(s32[3]{0:T(128)S(1)} %copy-done.13, f32[3,2]{1,0:T(4,128)S(1)} %copy.18.mix_ref, bf16[1,16,2,1500]{3,2,1,0:T(2,128)(2,1)S(1)} %bitcast.8, bf16[3,512]{1,0:T(4,128)(2,1)S(1)} %copy-done.7, f32[1,512]{1,0:T(1,128)S(1)} %bitcast.10, bf16[2,512]{1,0:T(2,128)(2,1)S(1)} %copy-done.9, ...), custom_call_target="tpu_custom_call" | custom-call | tf_op jit(solution)/shard_map/pallas_call | solution.py:226
  37.5 10.7 %all_to_all.10.x_ref = bf16[16,2,1500]{2,1,0:T(2,128)(2,1)} all-to-all(bf16[16,2,1500]{2,1,0:T(2,128)(2,1)S(1)} %bitcast.9), channel_id=1, replica_groups=mesh['groups'=2,'lon'=16] {'lon'}, dimensions={0} | all-to-all | bytes 192000 | tf_op jit(solution)/shard_map/all_to_all | solution.py:298
  48.2 1.6 %shard_map.165 = bf16[32,1500]{1,0:T(8,128)(2,1)} custom-call(bf16[16,2,1500]{2,1,0:T(2,128)(2,1)} %all_to_all.10.x_ref), custom_call_target="tpu_custom_call" | custom-call | tf_op jit(solution)/shard_map/pallas_call | solution.py:216
  (12 shorter events, 0.0 us)
Async XLA Ops:
  0.0 16.5 %copy-start.3 = (bf16[512,1024]{1,0:T(8,128)(2,1)S(1)}, bf16[512,1024]{1,0:T(8,128)(2,1)}, u32[]{:S(2)}) copy-start(bf16[512,1024]{1,0:T(8,128)(2,1)} %kv_ref.1) | copy-start | bytes 3145732
  1.7 14.8 %all-to-all-start = ((bf16[16,2,1500]{2,1,0:T(2,128)(2,1)}), bf16[16,2,1500]{2,1,0:T(2,128)(2,1)S(1)}, u32[]{:S(2)}, u32[]{:S(2)}) async-start(bf16[16,2,1500]{2,1,0:T(2,128)(2,1)} %shard_map.163), calls=%async_computation | async-start | bytes 196608 | tf_op jit(solution)/shard_map/all_to_all | solution.py:267
  16.5 1.6 %copy-start = (bf16[512,2048]{1,0:T(8,128)(2,1)S(1)}, bf16[512,2048]{1,0:T(8,128)(2,1)}, u32[]{:S(2)}) copy-start(bf16[512,2048]{1,0:T(8,128)(2,1)} %up_ref.1) | copy-start | bytes 6291460
  18.1 1.6 %copy-start.1 = (bf16[2048,512]{1,0:T(8,128)(2,1)S(1)}, bf16[2048,512]{1,0:T(8,128)(2,1)}, u32[]{:S(2)}) copy-start(bf16[2048,512]{1,0:T(8,128)(2,1)} %down_ref.1) | copy-start | bytes 6291460
  19.7 1.4 %copy-start.2 = (bf16[512,1536]{1,0:T(8,128)(2,1)S(1)}, bf16[512,1536]{1,0:T(8,128)(2,1)}, u32[]{:S(2)}) copy-start(bf16[512,1536]{1,0:T(8,128)(2,1)} %qkv_ref.1) | copy-start | bytes 4718596
  21.1 1.0 %copy-start.4 = (bf16[512,512]{1,0:T(8,128)(2,1)S(1)}, bf16[512,512]{1,0:T(8,128)(2,1)}, u32[]{:S(2)}) copy-start(bf16[512,512]{1,0:T(8,128)(2,1)} %pool_ref.1) | copy-start | bytes 1572868
  22.2 1.0 %copy-start.5 = (bf16[512,512]{1,0:T(8,128)(2,1)S(1)}, bf16[512,512]{1,0:T(8,128)(2,1)}, u32[]{:S(2)}) copy-start(bf16[512,512]{1,0:T(8,128)(2,1)} %proj_ref.1) | copy-start | bytes 1572868
  23.2 1.0 %copy-start.6 = (bf16[500,512]{1,0:T(8,128)(2,1)S(1)}, bf16[500,512]{1,0:T(8,128)(2,1)}, u32[]{:S(2)}) copy-start(bf16[500,512]{1,0:T(8,128)(2,1)} %embed_ref.1) | copy-start | bytes 1536004
  24.3 0.7 %copy-start.7 = (bf16[3,512]{1,0:T(4,128)(2,1)S(1)}, bf16[3,512]{1,0:T(4,128)(2,1)}, u32[]{:S(2)}) copy-start(bf16[3,512]{1,0:T(4,128)(2,1)} %level_embed_ref.1) | copy-start | bytes 9220
  24.9 0.7 %copy-start.8 = (f32[512]{0:T(512)S(1)}, f32[512]{0:T(512)}, u32[]{:S(2)}) copy-start(f32[512]{0:T(512)} %param.21) | copy-start | bytes 6148
  25.6 0.7 %copy-start.9 = (bf16[2,512]{1,0:T(2,128)(2,1)S(1)}, bf16[2,512]{1,0:T(2,128)(2,1)}, u32[]{:S(2)}) copy-start(bf16[2,512]{1,0:T(2,128)(2,1)} %latent_query_ref.1) | copy-start | bytes 6148
  26.3 0.7 %copy-start.10 = (f32[512]{0:T(512)S(1)}, f32[512]{0:T(512)}, u32[]{:S(2)}) copy-start(f32[512]{0:T(512)} %param.25) | copy-start | bytes 6148
  27.0 0.7 %copy-start.11 = (f32[512]{0:T(512)S(1)}, f32[512]{0:T(512)}, u32[]{:S(2)}) copy-start(f32[512]{0:T(512)} %param.28) | copy-start | bytes 6148
  27.7 0.7 %copy-start.12 = (f32[512]{0:T(512)S(1)}, f32[512]{0:T(512)}, u32[]{:S(2)}) copy-start(f32[512]{0:T(512)} %param.32) | copy-start | bytes 6148
  28.4 0.7 %copy-start.13 = (s32[3]{0:T(128)S(1)}, s32[3]{0:T(128)}, u32[]{:S(2)}) copy-start(s32[3]{0:T(128)} %ids_ref.1) | copy-start | bytes 40

commit v2 on v1

--- a/solution.py
+++ b/solution.py
@@ -22,6 +22,7 @@
 TOKENS = PATCHES * LATL
 HALF = D // 2
 PAIR = 2 * HEAD_DIM
+PARAMETERS = 16
 
 norm_eps = 1e-05
 head_eps = 1e-06
@@ -56,33 +57,57 @@
     return result
 
 
-def forecast_kernel(
-    windows,
-    ids_ref,
-    mix_ref,
-    x_ref,
-    level_embed_ref,
-    enc_gain_ref,
-    latent_query_ref,
-    attn_gain_ref,
-    mlp_gain_ref,
-    dec_gain_ref,
-    embed_ref,
-    kv_ref,
-    pool_ref,
-    qkv_ref,
-    proj_ref,
-    up_ref,
-    down_ref,
-    dec_ref,
-    out_ref,
-    state,
-    wide,
-):
+def forecast_kernel(windows, *refs):
+    parameters, (x_ref, out_ref) = refs[:PARAMETERS], refs[PARAMETERS : PARAMETERS + 2]
+    held = refs[PARAMETERS + 2 : 2 * PARAMETERS + 2]
+    state, wide, arrivals = refs[2 * PARAMETERS + 2 :]
+    (
+        ids_ref,
+        mix_ref,
+        level_embed_ref,
+        latent_query_ref,
+        enc_gain_ref,
+        embed_ref,
+        kv_ref,
+        pool_ref,
+        attn_gain_ref,
+        qkv_ref,
+        proj_ref,
+        mlp_gain_ref,
+        up_ref,
+        down_ref,
+        dec_gain_ref,
+        dec_ref,
+    ) = held
+    copies = {
+        id(there): pltpu.make_async_copy(here, there, arrivals.at[i])
+        for i, (here, there) in enumerate(zip(parameters, held))
+    }
+
+    def in_first_window(action):
+        if windows == 1:
+            action()
+        else:
+            pl.when(pl.program_id(0) == 0)(action)
+
+    def start_all():
+        for there in held:
+            copies[id(there)].start()
+
+    def wait_for(*wanted):
+        def action():
+            for there in wanted:
+                copies[id(there)].wait()
+
+        in_first_window(action)
+
+    in_first_window(start_all)
+    wait_for(ids_ref, mix_ref, level_embed_ref, latent_query_ref)
+
     table = level_embed_ref[...].astype(F32)
     rows = [table[i : i + 1] for i in range(LEV)]
     embeds = [picked(ids_ref[l], rows) for l in range(LEV)]
-    mixing = [[mix_ref[ids_ref[l], j] for j in range(LATL)] for l in range(LEV)]
+    mixing = [[mix_ref[j, ids_ref[l]] for j in range(LATL)] for l in range(LEV)]
     latent = latent_query_ref[...].astype(F32)
 
     row16 = iota((LATL * HEADS, D), 0)
@@ -115,13 +140,16 @@
     for l in range(LEV):
         state[l * PATCHES : (l + 1) * PATCHES, :] = arrived[:, l * PIN : (l + 1) * PIN]
 
-    def step(_, carry):
+    def step(first):
+        wait = wait_for if first else lambda *wanted: None
+        wait(enc_gain_ref, embed_ref)
         patches = state[...].astype(BF16)
         tokens = mm(patches, embed_ref[...])
         tokens = jnp.concatenate(
             [tokens[l * PATCHES : (l + 1) * PATCHES] + embeds[l] for l in range(LEV)], axis=0
         )
         tokens = layer_norm(tokens, enc_gain_ref[...]).astype(BF16)
+        wait(kv_ref)
         keyval = mm(tokens, kv_ref[...])
         keys = keyval[:, :D]
         values = keyval[:, D:].astype(BF16).astype(F32)
@@ -144,11 +172,13 @@
                 total = term if total is None else total + term
             pooled.append(total)
         pooled = jnp.concatenate(pooled, axis=0).astype(BF16)
+        wait(pool_ref)
         latents = mm(pooled, pool_ref[...])
         latents = jnp.concatenate(
             [latents[j * PATCHES : (j + 1) * PATCHES] + latent[j : j + 1] for j in range(LATL)],
             axis=0,
         )
+        wait(attn_gain_ref, qkv_ref)
         normed = layer_norm(latents, attn_gain_ref[...]).astype(BF16)
         projected = mm(normed, qkv_ref[...])
         halves = jnp.concatenate(
@@ -173,10 +203,14 @@
             weights = weights.astype(BF16)
             both = mm(weights, jnp.concatenate([value, half_ones], axis=1))
             mixed.append((both[:, :PAIR] / both[:, PAIR:]).astype(BF16))
+        wait(proj_ref)
         attended = latents + mm(jnp.concatenate(mixed, axis=1), proj_ref[...])
+        wait(mlp_gain_ref, up_ref)
         normed = layer_norm(attended, mlp_gain_ref[...]).astype(BF16)
         hidden = jax.nn.gelu(mm(normed, up_ref[...])).astype(BF16)
+        wait(down_ref)
         backbone = attended + mm(hidden, down_ref[...])
+        wait(dec_gain_ref, dec_ref)
         blended = jnp.concatenate(
             [
                 mixing[l][0] * backbone[:PATCHES] + mixing[l][1] * backbone[PATCHES:] + embeds[l]
@@ -185,10 +219,10 @@
             axis=0,
         )
         normed = layer_norm(blended, dec_gain_ref[...]).astype(BF16)
-        state[...] = (state[...] + mm(normed, dec_ref[...])).astype(BF16).astype(F32)
-        return carry
-
-    lax.fori_loop(0, STEPS, step, 0)
+        state[...] = (state[...] + mm_t(normed, dec_ref[...])).astype(BF16).astype(F32)
+
+    for turn_index in range(STEPS):
+        step(turn_index == 0)
     for l in range(LEV):
         wide[:, l * PIN : (l + 1) * PIN] = state[l * PATCHES : (l + 1) * PATCHES, :]
     out_ref[0] = wide[...].reshape(PATCHES // 2, 2, LEV * PIN).astype(BF16)
@@ -219,22 +253,26 @@
     )(array)
 
 
-def forecast(windows, arranged, ids, mix, *tensors):
-    vmem = pl.BlockSpec(memory_space=pltpu.VMEM)
-    smem = pl.BlockSpec(memory_space=pltpu.SMEM)
+def forecast(windows, arranged, *parameters):
     block = pl.BlockSpec((1,) + arranged.shape[1:], lambda i: (i, 0, 0, 0))
+    held = [
+        pltpu.SMEM(a.shape, a.dtype) if i < 2 else pltpu.VMEM(a.shape, a.dtype)
+        for i, a in enumerate(parameters)
+    ]
     return pl.pallas_call(
         functools.partial(forecast_kernel, windows),
         grid=(windows,),
-        in_specs=[smem, smem, block] + [vmem] * len(tensors),
+        in_specs=[pl.BlockSpec(memory_space=pl.ANY)] * PARAMETERS + [block],
         out_specs=block,
         out_shape=jax.ShapeDtypeStruct(arranged.shape, BF16),
-        scratch_shapes=[
+        scratch_shapes=held
+        + [
             pltpu.VMEM((LEV * PATCHES, PIN), F32),
             pltpu.VMEM((PATCHES, LEV * PIN), F32),
+            pltpu.SemaphoreType.DMA((PARAMETERS,)),
         ],
-        compiler_params=pltpu.CompilerParams(vmem_limit_bytes=40 * 1024 * 1024),
-    )(ids, mix, arranged, *tensors)
+        compiler_params=pltpu.CompilerParams(vmem_limit_bytes=56 * 1024 * 1024),
+    )(*parameters, arranged)
 
 
 def shards(
@@ -274,21 +312,21 @@
         bands,
         arranged,
         level_ids,
-        level_mix,
+        level_mix.T,
         level_embed,
+        latent_query,
         enc_gain.reshape(1, D),
-        latent_query,
-        attn_gain.reshape(1, D),
-        mlp_gain.reshape(1, D),
-        dec_gain.reshape(1, D),
         embed_weight,
         kv_weight,
         pool_out,
+        attn_gain.reshape(1, D),
         qkv_weight,
         attn_proj,
+        mlp_gain.reshape(1, D),
         mlp_up,
         mlp_down,
-        dec_weight,
+        dec_gain.reshape(1, D),
+        dec_weight.T,
     )
     if bands > 1:
         done = done.reshape(bands, ROW_PARTS, W_LAT, piece_cols, width).transpose(1, 0, 2, 3, 4)

time: 50.5 us -> 41 us (0.81)
  blocking collectives: 10.7 us -> 26.5 us
  local copies, waits for them, and re-layouts: 14.5 us -> 0 us
  starting transfers between devices: 7.39 us -> 0 us
  waiting for transfers between devices: 5.39 us -> 0 us
  Pallas kernels: 11.8 us -> 14.1 us
    all_to_all x0 -> x1, blocking collectives: none -> 14.9 us  [shards(): lax.all_to_all(outgoing, 'lon', split_axis=0, concat_axis=0, tiled=True)]
    unnamed x30 -> x0, local copies, waits for them, and re-layouts: 14.5 us -> none
    all_to_all x1 -> x0, starting transfers between devices: 7.39 us -> none  [shards(): lax.all_to_all(outgoing, 'lon', split_axis=0, concat_axis=0, tiled=True)]
    all_to_all x1 -> x0, waiting for transfers between devices: 5.39 us -> none  [shards(): lax.all_to_all(outgoing, 'lon', split_axis=0, concat_axis=0, tiled=True)]
    pallas_call x1, Pallas kernels: 8.52 us -> 10.9 us  [forecast(): pl.pallas_call(functools.partial(forecast_kernel, windows), grid=(windows...]
    all_to_all x1, blocking collectives: 10.7 us -> 11.6 us  [shards(): home = lax.all_to_all(done, 'lon', split_axis=0, concat_axis=0, tiled=True)]
  transfers between devices with their start and end apart: 1 -> 0, of which waited for: 1 -> 0; matrix products, arithmetic and copies ran while one was open for 4% -> 0% of each run, Pallas kernels for 0% -> 0%
where the time goes in v2:
time: 41 us; the launch traced here: 40.6 us
  blocking collectives  26.5 us (65%)
  Pallas kernels  14.1 us (34%)
    all_to_all x1, blocking collectives, shards(): lax.all_to_all(outgoing, 'lon', split_axis=0, concat_axis=0, tiled=True)  14.9 us
    all_to_all x1, blocking collectives, shards(): home = lax.all_to_all(done, 'lon', split_axis=0, concat_axis=0, tiled=True)  11.6 us
    pallas_call x1, Pallas kernels, forecast(): pl.pallas_call(functools.partial(forecast_kernel, windows), grid=(windows...  10.9 us
    pallas_call x2, Pallas kernels, turn(): pl.pallas_call(functools.partial(turn_kernel, step, direction), out_shape...  3.21 us

profile of v2, /device:TPU:0, one launch (start us, length us, event | category | flops | bytes accessed | tf_op | source)
XLA Modules:
  0.0 40.6 jit_solution(4770432705707440282)
XLA Ops:
  0.0 1.6 %shard_map.163 = bf16[16,2,1500]{2,1,0:T(2,128)(2,1)} custom-call(bf16[32,1500]{1,0:T(8,128)(2,1)} %bitcast.13), custom_call_target="tpu_custom_call" | custom-call | tf_op jit(solution)/shard_map/pallas_call | solution.py:250
  1.6 14.9 %all_to_all.10 = bf16[16,2,1500]{2,1,0:T(2,128)(2,1)} all-to-all(bf16[16,2,1500]{2,1,0:T(2,128)(2,1)} %shard_map.163), channel_id=1, replica_groups=mesh['groups'=2,'lon'=16] {'lon'}, dimensions={0} | all-to-all | bytes 192000 | tf_op jit(solution)/shard_map/all_to_all | solution.py:305
  16.5 10.9 %shard_map.164 = bf16[1,16,2,1500]{3,2,1,0:T(2,128)(2,1)} custom-call(s32[3]{0:T(128)} %refs_0_.1, f32[2,3]{1,0:T(2,128)} %bitcast.18, bf16[3,512]{1,0:T(4,128)(2,1)} %refs_2_.1, bf16[2,512]{1,0:T(2,128)(2,1)} %refs_3_.1, f32[1,512]{1,0:T(1,128)} %bitcast.14, bf16[500,512]{1,0:T(8,128)(2,1)} %refs_5_.1, bf16[512,1024]{1,0:T(8,128)(2,1)} %refs_6_.1, ...), custom_call_target="tpu_custom_call" | custom-call | tf_op jit(solution)/shard_map/pallas_call | solution.py:262
  27.5 11.6 %all_to_all.11.x_ref = bf16[16,2,1500]{2,1,0:T(2,128)(2,1)} all-to-all(bf16[16,2,1500]{2,1,0:T(2,128)(2,1)} %bitcast.12), channel_id=1, replica_groups=mesh['groups'=2,'lon'=16] {'lon'}, dimensions={0} | all-to-all | bytes 192000 | tf_op jit(solution)/shard_map/all_to_all | solution.py:336
  39.1 1.6 %shard_map.165 = bf16[32,1500]{1,0:T(8,128)(2,1)} custom-call(bf16[16,2,1500]{2,1,0:T(2,128)(2,1)} %all_to_all.11.x_ref), custom_call_target="tpu_custom_call" | custom-call | tf_op jit(solution)/shard_map/pallas_call | solution.py:250

commit v3 on v1

--- a/solution.py
+++ b/solution.py
@@ -22,6 +22,7 @@
 TOKENS = PATCHES * LATL
 HALF = D // 2
 PAIR = 2 * HEAD_DIM
+PARAMETERS = 16
 
 norm_eps = 1e-05
 head_eps = 1e-06
@@ -56,33 +57,32 @@
     return result
 
 
-def forecast_kernel(
-    windows,
-    ids_ref,
-    mix_ref,
-    x_ref,
-    level_embed_ref,
-    enc_gain_ref,
-    latent_query_ref,
-    attn_gain_ref,
-    mlp_gain_ref,
-    dec_gain_ref,
-    embed_ref,
-    kv_ref,
-    pool_ref,
-    qkv_ref,
-    proj_ref,
-    up_ref,
-    down_ref,
-    dec_ref,
-    out_ref,
-    state,
-    wide,
-):
+def forecast_kernel(windows, blocks, *refs):
+    (
+        ids_ref,
+        mix_ref,
+        level_embed_ref,
+        latent_query_ref,
+        enc_gain_ref,
+        attn_gain_ref,
+        mlp_gain_ref,
+        dec_gain_ref,
+        embed_ref,
+        kv_ref,
+        pool_ref,
+        qkv_ref,
+        proj_ref,
+        up_ref,
+        down_ref,
+        dec_ref,
+    ) = refs[:PARAMETERS]
+    refs = refs[PARAMETERS:]
+    x_refs, out_refs, (state, wide) = refs[:blocks], refs[blocks : 2 * blocks], refs[2 * blocks :]
+
     table = level_embed_ref[...].astype(F32)
     rows = [table[i : i + 1] for i in range(LEV)]
     embeds = [picked(ids_ref[l], rows) for l in range(LEV)]
-    mixing = [[mix_ref[ids_ref[l], j] for j in range(LATL)] for l in range(LEV)]
+    mixing = [[mix_ref[j, ids_ref[l]] for j in range(LATL)] for l in range(LEV)]
     latent = latent_query_ref[...].astype(F32)
 
     row16 = iota((LATL * HEADS, D), 0)
@@ -111,11 +111,14 @@
     cut = jnp.where(pl.program_id(0) == windows - 1, 1, 0)
     allowed = jnp.where((row_bit - lane_bit) * cut == 0, 1.0, 0.0)
 
-    arrived = x_ref[0].astype(F32).reshape(PATCHES, LEV * PIN)
+    if blocks == 1:
+        arrived = x_refs[0][0].astype(F32).reshape(PATCHES, LEV * PIN)
+    else:
+        arrived = jnp.concatenate([x_ref[...].astype(F32) for x_ref in x_refs], axis=0)
     for l in range(LEV):
         state[l * PATCHES : (l + 1) * PATCHES, :] = arrived[:, l * PIN : (l + 1) * PIN]
 
-    def step(_, carry):
+    def step():
         patches = state[...].astype(BF16)
         tokens = mm(patches, embed_ref[...])
         tokens = jnp.concatenate(
@@ -185,13 +188,18 @@
             axis=0,
         )
         normed = layer_norm(blended, dec_gain_ref[...]).astype(BF16)
-        state[...] = (state[...] + mm(normed, dec_ref[...])).astype(BF16).astype(F32)
-        return carry
-
-    lax.fori_loop(0, STEPS, step, 0)
+        state[...] = (state[...] + mm_t(normed, dec_ref[...])).astype(BF16).astype(F32)
+
+    for _ in range(STEPS):
+        step()
     for l in range(LEV):
         wide[:, l * PIN : (l + 1) * PIN] = state[l * PATCHES : (l + 1) * PATCHES, :]
-    out_ref[0] = wide[...].reshape(PATCHES // 2, 2, LEV * PIN).astype(BF16)
+    if blocks == 1:
+        out_refs[0][0] = wide[...].reshape(out_refs[0].shape[1:]).astype(BF16)
+    else:
+        size = PATCHES // blocks
+        for k in range(blocks):
+            out_refs[k][...] = wide[k * size : (k + 1) * size].astype(BF16)
 
 
 def turn_kernel(step, direction, x_ref, out_ref):
@@ -219,22 +227,81 @@
     )(array)
 
 
-def forecast(windows, arranged, ids, mix, *tensors):
+def scatter_kernel(devices, lag, x_ref, *refs):
+    out_refs, apart = refs[:devices], refs[devices]
+    me = lax.axis_index("lon")
+    shift = jnp.where(me < lag, 1, 0)
+    apart[...] = x_ref[...].astype(F32).reshape(apart.shape)
+    for k in range(devices):
+        place = lax.rem((me ^ k) + shift, devices)
+        out_refs[k][...] = apart[place].astype(BF16)
+
+
+def gather_kernel(devices, lag, *refs):
+    x_refs, (out_ref, apart) = refs[:devices], refs[devices:]
+    me = lax.axis_index("lon")
+    shift = jnp.where(me < lag, 1, 0)
+    for k in range(devices):
+        place = lax.rem((me ^ k) + shift, devices)
+        apart[place] = x_refs[k][...].astype(F32)
+    out_ref[...] = apart[...].reshape(out_ref.shape).astype(BF16)
+
+
+def load_kernel(*refs):
+    count = (len(refs) - 2) // 2
+    here, there, arrivals = refs[:count], refs[count + 1 : -1], refs[-1]
+    copies = [
+        pltpu.make_async_copy(here[i], there[i], arrivals.at[i]) for i in range(count)
+    ]
+    for copy in copies:
+        copy.start()
+    for copy in copies:
+        copy.wait()
+
+
+def load(after, parameters):
+    far = pl.BlockSpec(memory_space=pl.ANY)
+    return pl.pallas_call(
+        load_kernel,
+        in_specs=[far] * (len(parameters) + 1),
+        out_specs=[pl.BlockSpec(memory_space=pltpu.VMEM)] * len(parameters),
+        out_shape=[pltpu.VMEM(a.shape, a.dtype) for a in parameters],
+        scratch_shapes=[pltpu.SemaphoreType.DMA((len(parameters),))],
+        compiler_params=pltpu.CompilerParams(vmem_limit_bytes=55 * 1024 * 1024),
+        cost_estimate=pl.CostEstimate(
+            flops=0,
+            bytes_accessed=sum(a.size * a.dtype.itemsize for a in parameters),
+            transcendentals=0,
+        ),
+    )(*parameters, after)
+
+
+def exchange(blocks):
+    devices = len(blocks)
+    return list(blocks[:1]) + [
+        lax.ppermute(blocks[k], "lon", [(i, i ^ k) for i in range(devices)])
+        for k in range(1, devices)
+    ]
+
+
+def forecast(windows, arranged, *parameters):
+    blocks = len(arranged)
+    shape = arranged[0].shape
     vmem = pl.BlockSpec(memory_space=pltpu.VMEM)
     smem = pl.BlockSpec(memory_space=pltpu.SMEM)
-    block = pl.BlockSpec((1,) + arranged.shape[1:], lambda i: (i, 0, 0, 0))
+    block = pl.BlockSpec((1,) + shape[1:], lambda i: (i, 0, 0, 0)) if blocks == 1 else vmem
     return pl.pallas_call(
-        functools.partial(forecast_kernel, windows),
+        functools.partial(forecast_kernel, windows, blocks),
         grid=(windows,),
-        in_specs=[smem, smem, block] + [vmem] * len(tensors),
-        out_specs=block,
-        out_shape=jax.ShapeDtypeStruct(arranged.shape, BF16),
+        in_specs=[smem] * 2 + [vmem] * (PARAMETERS - 2) + [block] * blocks,
+        out_specs=[block] * blocks,
+        out_shape=[jax.ShapeDtypeStruct(shape, BF16)] * blocks,
         scratch_shapes=[
             pltpu.VMEM((LEV * PATCHES, PIN), F32),
             pltpu.VMEM((PATCHES, LEV * PIN), F32),
         ],
-        compiler_params=pltpu.CompilerParams(vmem_limit_bytes=40 * 1024 * 1024),
-    )(ids, mix, arranged, *tensors)
+        compiler_params=pltpu.CompilerParams(vmem_limit_bytes=24 * 1024 * 1024),
+    )(*parameters, *arranged)
 
 
 def shards(
@@ -263,21 +330,11 @@
     lat_count = devices // ROW_PARTS
     bands = lat_count // W_LAT
     cut = (W_LON // 2 // piece_cols) * lat_count
-    outgoing = turn(fields.reshape(local_count, width), (devices, piece_cols, width), cut, 1)
-    got = lax.all_to_all(outgoing, "lon", split_axis=0, concat_axis=0, tiled=True)
-    if bands > 1:
-        got = got.reshape(ROW_PARTS, lat_count, piece_cols, width)
-        got = jnp.roll(got, -(W_LAT // 2), axis=1)
-        got = got.reshape(ROW_PARTS, bands, W_LAT, piece_cols, width).transpose(1, 0, 2, 3, 4)
-    arranged = got.reshape(bands, ROW_PARTS * W_LAT, piece_cols, width)
-    done = forecast(
-        bands,
-        arranged,
-        level_ids,
-        level_mix,
+    scalars = (level_ids, level_mix.T)
+    tensors = (
         level_embed,
+        latent_query,
         enc_gain.reshape(1, D),
-        latent_query,
         attn_gain.reshape(1, D),
         mlp_gain.reshape(1, D),
         dec_gain.reshape(1, D),
@@ -288,13 +345,35 @@
         attn_proj,
         mlp_up,
         mlp_down,
-        dec_weight,
+        dec_weight.T,
     )
-    if bands > 1:
-        done = done.reshape(bands, ROW_PARTS, W_LAT, piece_cols, width).transpose(1, 0, 2, 3, 4)
-        done = done.reshape(ROW_PARTS, lat_count, piece_cols, width)
-        done = jnp.roll(done, W_LAT // 2, axis=1)
-    done = done.reshape(devices, piece_cols, width)
+    if devices == ROW_PARTS * W_LAT:
+        piece = jax.ShapeDtypeStruct((piece_cols, width), BF16)
+        apart = pltpu.VMEM((devices, piece_cols, width), F32)
+        outgoing = pl.pallas_call(
+            functools.partial(scatter_kernel, devices, cut),
+            out_shape=[piece] * devices,
+            scratch_shapes=[apart],
+        )(fields.reshape(local_count, width))
+        held = load(outgoing[0], tensors)
+        done = forecast(1, exchange(outgoing), *scalars, *held)
+        home = pl.pallas_call(
+            functools.partial(gather_kernel, devices, cut),
+            out_shape=jax.ShapeDtypeStruct((local_count, width), BF16),
+            scratch_shapes=[apart],
+        )(*exchange(done))
+        return home.reshape(fields.shape)
+    outgoing = turn(fields.reshape(local_count, width), (devices, piece_cols, width), cut, 1)
+    held = load(outgoing, tensors)
+    got = lax.all_to_all(outgoing, "lon", split_axis=0, concat_axis=0, tiled=True)
+    got = got.reshape(ROW_PARTS, lat_count, piece_cols, width)
+    got = jnp.roll(got, -(W_LAT // 2), axis=1)
+    got = got.reshape(ROW_PARTS, bands, W_LAT, piece_cols, width).transpose(1, 0, 2, 3, 4)
+    arranged = got.reshape(bands, ROW_PARTS * W_LAT, piece_cols, width)
+    (done,) = forecast(bands, [arranged], *scalars, *held)
+    done = done.reshape(bands, ROW_PARTS, W_LAT, piece_cols, width).transpose(1, 0, 2, 3, 4)
+    done = done.reshape(ROW_PARTS, lat_count, piece_cols, width)
+    done = jnp.roll(done, W_LAT // 2, axis=1).reshape(devices, piece_cols, width)
     home = lax.all_to_all(done, "lon", split_axis=0, concat_axis=0, tiled=True)
     return turn(home, (local_count, width), cut, -1).reshape(fields.shape)
 

time: 50.5 us -> 65.4 us (1.30)
  starting transfers between devices: 7.39 us -> 42.6 us
  local copies, waits for them, and re-layouts: 14.5 us -> 1.11 us
  blocking collectives: 10.7 us -> 0 us
  Pallas kernels: 11.8 us -> 15.4 us
    ppermute x0 -> x30, starting transfers between devices: none -> 42.6 us  [exchange(): lax.ppermute(blocks[k], 'lon', [(i, i ^ k) for i in range(devices)])]
    unnamed x30 -> x38, local copies, waits for them, and re-layouts: 14.5 us -> 1.11 us
    all_to_all x1 -> x0, blocking collectives: 10.7 us -> none  [shards(): home = lax.all_to_all(done, 'lon', split_axis=0, concat_axis=0, tiled=True)]
    all_to_all x1 -> x0, starting transfers between devices: 7.39 us -> none  [shards(): lax.all_to_all(outgoing, 'lon', split_axis=0, concat_axis=0, tiled=True)]
    ppermute x0 -> x30, waiting for transfers between devices: none -> 5.97 us  [exchange(): lax.ppermute(blocks[k], 'lon', [(i, i ^ k) for i in range(devices)])]
    all_to_all x1 -> x0, waiting for transfers between devices: 5.39 us -> none  [shards(): lax.all_to_all(outgoing, 'lon', split_axis=0, concat_axis=0, tiled=True)]
    pallas_call x3 -> x4, Pallas kernels: 11.8 us -> 15.4 us  [the longest x1 8.47 us: forecast(): pl.pallas_call(functools.partial(forecast_kernel, windows, blocks), grid=...]
  transfers between devices with their start and end apart: 1 -> 30, of which waited for: 1 -> 3; matrix products, arithmetic and copies ran while one was open for 4% -> 0% of each run, Pallas kernels for 0% -> 6%
where the time goes in v3:
time: 65.4 us; the launch traced here: 65.2 us
  starting transfers between devices  42.6 us (65%)
  Pallas kernels  15.4 us (24%)
  waiting for transfers between devices  5.97 us (9%)
  local copies, waits for them, and re-layouts  1.11 us (2%)
    ppermute x30, starting transfers between devices, exchange(): lax.ppermute(blocks[k], 'lon', [(i, i ^ k) for i in range(devices)])  42.6 us
    pallas_call x1, Pallas kernels, forecast(): pl.pallas_call(functools.partial(forecast_kernel, windows, blocks), grid=...  8.47 us
    ppermute x30, waiting for transfers between devices, exchange(): lax.ppermute(blocks[k], 'lon', [(i, i ^ k) for i in range(devices)])  5.97 us
    pallas_call x1, Pallas kernels, load(): pl.pallas_call(load_kernel, in_specs=[far] * (len(parameters) + 1), out_s...  3.74 us
    pallas_call x1, Pallas kernels, shards(): pl.pallas_call(functools.partial(scatter_kernel, devices, cut), out_shape...  1.6 us
    pallas_call x1, Pallas kernels, shards(): pl.pallas_call(functools.partial(gather_kernel, devices, cut), out_shape=...  1.56 us
  transfers between devices with their start and end apart: 30, of which 3 were waited for; matrix products, arithmetic and copies ran while one was open for 0% of the time, Pallas kernels for 6%

profile of v3, /device:TPU:0, one launch (start us, length us, event | category | flops | bytes accessed | tf_op | source)
XLA Modules:
  0.0 65.2 jit_solution(6339626885417297945)
XLA Ops:
  0.0 1.6 %shard_map.163 = (bf16[2,1500]{1,0:T(2,128)(2,1)}, bf16[2,1500]{1,0:T(2,128)(2,1)}, bf16[2,1500]{1,0:T(2,128)(2,1)}, bf16[2,1500]{1,0:T(2,128)(2,1)}, bf16[2,150...) custom-call(bf16[32,1500]{1,0:T(8,128)(2,1)} %bitcast.10), custom_call_target="tpu_custom_call" | custom-call | tf_op jit(solution)/shard_map/pallas_call | solution.py:353
  2.1 2.6 %collective-permute-start.1 = (bf16[2,1500]{1,0:T(2,128)(2,1)}, bf16[2,1500]{1,0:T(2,128)(2,1)S(1)}, u32[]{:S(2)}, u32[]{:S(2)}) collective-permute-start(bf16[2,1500]{1,0:T(2,128)(2,1)} %get-tuple-element.67), channel_id=1, source_target_pairs={{0,2},{1,3},{2,0},{3,1},{4,6},{5,7},{6,4},{7,5},{8,10},{9,11},{10,... | collective-permute-start | bytes 18008 | tf_op jit(solution)/shard_map/ppermute | solution.py:282
  4.8 1.8 %collective-permute-start.3 = (bf16[2,1500]{1,0:T(2,128)(2,1)}, bf16[2,1500]{1,0:T(2,128)(2,1)S(1)}, u32[]{:S(2)}, u32[]{:S(2)}) collective-permute-start(bf16[2,1500]{1,0:T(2,128)(2,1)} %get-tuple-element.69), channel_id=1, source_target_pairs={{0,4},{1,5},{2,6},{3,7},{4,0},{5,1},{6,2},{7,3},{8,12},{9,13},{10,... | collective-permute-start | bytes 18008 | tf_op jit(solution)/shard_map/ppermute | solution.py:282
  6.6 2.6 %collective-permute-start.5 = (bf16[2,1500]{1,0:T(2,128)(2,1)}, bf16[2,1500]{1,0:T(2,128)(2,1)S(1)}, u32[]{:S(2)}, u32[]{:S(2)}) collective-permute-start(bf16[2,1500]{1,0:T(2,128)(2,1)} %get-tuple-element.71), channel_id=1, source_target_pairs={{0,6},{1,7},{2,4},{3,5},{4,2},{5,3},{6,0},{7,1},{8,14},{9,15},{10,... | collective-permute-start | bytes 18008 | tf_op jit(solution)/shard_map/ppermute | solution.py:282
  9.3 2.6 %collective-permute-start.7 = (bf16[2,1500]{1,0:T(2,128)(2,1)}, bf16[2,1500]{1,0:T(2,128)(2,1)S(1)}, u32[]{:S(2)}, u32[]{:S(2)}) collective-permute-start(bf16[2,1500]{1,0:T(2,128)(2,1)} %get-tuple-element.73), channel_id=1, source_target_pairs={{0,8},{1,9},{2,10},{3,11},{4,12},{5,13},{6,14},{7,15},{8,0},{9,1},... | collective-permute-start | bytes 18008 | tf_op jit(solution)/shard_map/ppermute | solution.py:282
  12.0 3.5 %collective-permute-start.9 = (bf16[2,1500]{1,0:T(2,128)(2,1)}, bf16[2,1500]{1,0:T(2,128)(2,1)S(1)}, u32[]{:S(2)}, u32[]{:S(2)}) collective-permute-start(bf16[2,1500]{1,0:T(2,128)(2,1)} %get-tuple-element.75), channel_id=1, source_target_pairs={{0,10},{1,11},{2,8},{3,9},{4,14},{5,15},{6,12},{7,13},{8,2},{9,3},... | collective-permute-start | bytes 18008 | tf_op jit(solution)/shard_map/ppermute | solution.py:282
  15.7 3.5 %collective-permute-start.11 = (bf16[2,1500]{1,0:T(2,128)(2,1)}, bf16[2,1500]{1,0:T(2,128)(2,1)S(1)}, u32[]{:S(2)}, u32[]{:S(2)}) collective-permute-start(bf16[2,1500]{1,0:T(2,128)(2,1)} %get-tuple-element.77), channel_id=1, source_target_pairs={{0,12},{1,13},{2,14},{3,15},{4,8},{5,9},{6,10},{7,11},{8,4},{9,5},... | collective-permute-start | bytes 18008 | tf_op jit(solution)/shard_map/ppermute | solution.py:282
  19.2 4.4 %collective-permute-start.13 = (bf16[2,1500]{1,0:T(2,128)(2,1)}, bf16[2,1500]{1,0:T(2,128)(2,1)S(1)}, u32[]{:S(2)}, u32[]{:S(2)}) collective-permute-start(bf16[2,1500]{1,0:T(2,128)(2,1)} %get-tuple-element.79), channel_id=1, source_target_pairs={{0,14},{1,15},{2,12},{3,13},{4,10},{5,11},{6,8},{7,9},{8,6},{9,7},... | collective-permute-start | bytes 18008 | tf_op jit(solution)/shard_map/ppermute | solution.py:282
  23.8 3.7 %shard_map.164 = (bf16[3,512]{1,0:T(4,128)(2,1)S(1)}, bf16[2,512]{1,0:T(2,128)(2,1)S(1)}, f32[1,512]{1,0:T(1,128)S(1)}, f32[1,512]{1,0:T(1,128)S(1)}, f32[1,512]...) custom-call(bf16[3,512]{1,0:T(4,128)(2,1)} %refs_0_.2, ...), custom_call_target="tpu_custom_call" | custom-call | bytes 8901632 | tf_op jit(solution)/shard_map/pallas_call | solution.py:264
  27.6 2.0 %collective-permute-done.14.refs_31_ = bf16[2,1500]{1,0:T(2,128)(2,1)S(1)} collective-permute-done((bf16[2,1500]{1,0:T(2,128)(2,1)}, bf16[2,1500]{1,0:T(2,128)(2,1)S(1)}, u32[]{:S(2)}, u32[]{:S(2)}) %collective-permute-start.14) | collective-permute-done | bytes 6032 | tf_op jit(solution)/shard_map/ppermute | solution.py:282
  29.6 8.5 %shard_map.165 = (bf16[2,1500]{1,0:T(2,128)(2,1)S(1)}, bf16[2,1500]{1,0:T(2,128)(2,1)S(1)}, bf16[2,1500]{1,0:T(2,128)(2,1)S(1)}, bf16[2,1500]{1,0:T(2,128)(2,1)S...) custom-call(s32[3]{0:T(128)S(1)} %copy-done.3, ...), custom_call_target="tpu_custom_call" | custom-call | tf_op jit(solution)/shard_map/pallas_call | solution.py:293
  39.4 1.2 %collective-permute-start.17 = (bf16[2,1500]{1,0:T(2,128)(2,1)S(1)}, bf16[2,1500]{1,0:T(2,128)(2,1)S(1)}, u32[]{:S(2)}, u32[]{:S(2)}) collective-permute-start(bf16[2,1500]{1,0:T(2,128)(2,1)S(1)} %get-tuple-element.84), channel_id=1, source_target_pairs={{0,3},{1,2},{2,1},{3,0},{4,7},{5,6},{6,5},{7,4},{8,11},{9,10},{10,... | collective-permute-start | bytes 18008 | tf_op jit(solution)/shard_map/ppermute | solution.py:282
  40.6 1.8 %collective-permute-start.19 = (bf16[2,1500]{1,0:T(2,128)(2,1)S(1)}, bf16[2,1500]{1,0:T(2,128)(2,1)S(1)}, u32[]{:S(2)}, u32[]{:S(2)}) collective-permute-start(bf16[2,1500]{1,0:T(2,128)(2,1)S(1)} %get-tuple-element.86), channel_id=1, source_target_pairs={{0,5},{1,4},{2,7},{3,6},{4,1},{5,0},{6,3},{7,2},{8,13},{9,12},{10,... | collective-permute-start | bytes 18008 | tf_op jit(solution)/shard_map/ppermute | solution.py:282
  42.6 2.3 %collective-permute-start.21 = (bf16[2,1500]{1,0:T(2,128)(2,1)S(1)}, bf16[2,1500]{1,0:T(2,128)(2,1)S(1)}, u32[]{:S(2)}, u32[]{:S(2)}) collective-permute-start(bf16[2,1500]{1,0:T(2,128)(2,1)S(1)} %get-tuple-element.88), channel_id=1, source_target_pairs={{0,7},{1,6},{2,5},{3,4},{4,3},{5,2},{6,1},{7,0},{8,15},{9,14},{10,... | collective-permute-start | bytes 18008 | tf_op jit(solution)/shard_map/ppermute | solution.py:282
  45.6 2.1 %collective-permute-start.23 = (bf16[2,1500]{1,0:T(2,128)(2,1)S(1)}, bf16[2,1500]{1,0:T(2,128)(2,1)S(1)}, u32[]{:S(2)}, u32[]{:S(2)}) collective-permute-start(bf16[2,1500]{1,0:T(2,128)(2,1)S(1)} %get-tuple-element.90), channel_id=1, source_target_pairs={{0,9},{1,8},{2,11},{3,10},{4,13},{5,12},{6,15},{7,14},{8,1},{9,0},... | collective-permute-start | bytes 18008 | tf_op jit(solution)/shard_map/ppermute | solution.py:282
  47.7 1.4 %collective-permute-start.24 = (bf16[2,1500]{1,0:T(2,128)(2,1)S(1)}, bf16[2,1500]{1,0:T(2,128)(2,1)S(1)}, u32[]{:S(2)}, u32[]{:S(2)}) collective-permute-start(bf16[2,1500]{1,0:T(2,128)(2,1)S(1)} %get-tuple-element.91), channel_id=1, source_target_pairs={{0,10},{1,11},{2,8},{3,9},{4,14},{5,15},{6,12},{7,13},{8,2},{9,3},... | collective-permute-start | bytes 18008 | tf_op jit(solution)/shard_map/ppermute | solution.py:282
  49.1 2.1 %collective-permute-start.25 = (bf16[2,1500]{1,0:T(2,128)(2,1)S(1)}, bf16[2,1500]{1,0:T(2,128)(2,1)S(1)}, u32[]{:S(2)}, u32[]{:S(2)}) collective-permute-start(bf16[2,1500]{1,0:T(2,128)(2,1)S(1)} %get-tuple-element.92), channel_id=1, source_target_pairs={{0,11},{1,10},{2,9},{3,8},{4,15},{5,14},{6,13},{7,12},{8,3},{9,2},... | collective-permute-start | bytes 18008 | tf_op jit(solution)/shard_map/ppermute | solution.py:282
  51.2 1.4 %collective-permute-start.26 = (bf16[2,1500]{1,0:T(2,128)(2,1)S(1)}, bf16[2,1500]{1,0:T(2,128)(2,1)S(1)}, u32[]{:S(2)}, u32[]{:S(2)}) collective-permute-start(bf16[2,1500]{1,0:T(2,128)(2,1)S(1)} %get-tuple-element.93), channel_id=1, source_target_pairs={{0,12},{1,13},{2,14},{3,15},{4,8},{5,9},{6,10},{7,11},{8,4},{9,5},... | collective-permute-start | bytes 18008 | tf_op jit(solution)/shard_map/ppermute | solution.py:282
  52.6 2.2 %collective-permute-start.27 = (bf16[2,1500]{1,0:T(2,128)(2,1)S(1)}, bf16[2,1500]{1,0:T(2,128)(2,1)S(1)}, u32[]{:S(2)}, u32[]{:S(2)}) collective-permute-start(bf16[2,1500]{1,0:T(2,128)(2,1)S(1)} %get-tuple-element.94), channel_id=1, source_target_pairs={{0,13},{1,12},{2,15},{3,14},{4,9},{5,8},{6,11},{7,10},{8,5},{9,4},... | collective-permute-start | bytes 18008 | tf_op jit(solution)/shard_map/ppermute | solution.py:282
  54.8 2.5 %collective-permute-start.28 = (bf16[2,1500]{1,0:T(2,128)(2,1)S(1)}, bf16[2,1500]{1,0:T(2,128)(2,1)S(1)}, u32[]{:S(2)}, u32[]{:S(2)}) collective-permute-start(bf16[2,1500]{1,0:T(2,128)(2,1)S(1)} %get-tuple-element.95), channel_id=1, source_target_pairs={{0,14},{1,15},{2,12},{3,13},{4,10},{5,11},{6,8},{7,9},{8,6},{9,7},... | collective-permute-start | bytes 18008 | tf_op jit(solution)/shard_map/ppermute | solution.py:282
  57.3 1.9 %collective-permute-start.29 = (bf16[2,1500]{1,0:T(2,128)(2,1)S(1)}, bf16[2,1500]{1,0:T(2,128)(2,1)S(1)}, u32[]{:S(2)}, u32[]{:S(2)}) collective-permute-start(bf16[2,1500]{1,0:T(2,128)(2,1)S(1)} %get-tuple-element.96), channel_id=1, source_target_pairs={{0,15},{1,14},{2,13},{3,12},{4,11},{5,10},{6,9},{7,8},{8,7},{9,6},... | collective-permute-start | bytes 18008 | tf_op jit(solution)/shard_map/ppermute | solution.py:282
  59.2 1.9 %collective-permute-done.28.refs_14_ = bf16[2,1500]{1,0:T(2,128)(2,1)S(1)} collective-permute-done((bf16[2,1500]{1,0:T(2,128)(2,1)S(1)}, bf16[2,1500]{1,0:T(2,128)(2,1)S(1)}, u32[]{:S(2)}, u32[]{:S(2)}) %collective-permute-start.28) | collective-permute-done | bytes 6032 | tf_op jit(solution)/shard_map/ppermute | solution.py:282
  61.1 1.9 %collective-permute-done.29.refs_15_ = bf16[2,1500]{1,0:T(2,128)(2,1)S(1)} collective-permute-done((bf16[2,1500]{1,0:T(2,128)(2,1)S(1)}, bf16[2,1500]{1,0:T(2,128)(2,1)S(1)}, u32[]{:S(2)}, u32[]{:S(2)}) %collective-permute-start.29) | collective-permute-done | bytes 6032 | tf_op jit(solution)/shard_map/ppermute | solution.py:282
  63.7 1.6 %shard_map.166 = bf16[32,1500]{1,0:T(8,128)(2,1)} custom-call(bf16[2,1500]{1,0:T(2,128)(2,1)} %copy-done.1, bf16[2,1500]{1,0:T(2,128)(2,1)} %copy-done.4, bf16[2,1500]{1,0:T(2,128)(2,1)} %copy-done.5, bf16[2,1500]{1,0:T(2,128)(2,1)} %copy-done.6, bf16[2,1500]{1,0:T(2,128)(2,1)} %copy-done.7, bf16[2,1500]{1,0:T(2,128)(2,1)} %copy-done.8, ...), custom_call_target="tpu_custom_call" | custom-call | tf_op jit(solution)/shard_map/pallas_call | solution.py:360
  (78 shorter events, 3.7 us)
Async XLA Ops:
  2.1 7.1 %collective-permute-start.1 = (bf16[2,1500]{1,0:T(2,128)(2,1)}, bf16[2,1500]{1,0:T(2,128)(2,1)S(1)}, u32[]{:S(2)}, u32[]{:S(2)}) collective-permute-start(bf16[2,1500]{1,0:T(2,128)(2,1)} %get-tuple-element.67), channel_id=1, source_target_pairs={{0,2},{1,3},{2,0},{3,1},{4,6},{5,7},{6,4},{7,5},{8,10},{9,11},{10,... | collective-permute-start | bytes 18008 | tf_op jit(solution)/shard_map/ppermute | solution.py:282
  4.8 7.2 %collective-permute-start.3 = (bf16[2,1500]{1,0:T(2,128)(2,1)}, bf16[2,1500]{1,0:T(2,128)(2,1)S(1)}, u32[]{:S(2)}, u32[]{:S(2)}) collective-permute-start(bf16[2,1500]{1,0:T(2,128)(2,1)} %get-tuple-element.69), channel_id=1, source_target_pairs={{0,4},{1,5},{2,6},{3,7},{4,0},{5,1},{6,2},{7,3},{8,12},{9,13},{10,... | collective-permute-start | bytes 18008 | tf_op jit(solution)/shard_map/ppermute | solution.py:282
  6.6 9.0 %collective-permute-start.5 = (bf16[2,1500]{1,0:T(2,128)(2,1)}, bf16[2,1500]{1,0:T(2,128)(2,1)S(1)}, u32[]{:S(2)}, u32[]{:S(2)}) collective-permute-start(bf16[2,1500]{1,0:T(2,128)(2,1)} %get-tuple-element.71), channel_id=1, source_target_pairs={{0,6},{1,7},{2,4},{3,5},{4,2},{5,3},{6,0},{7,1},{8,14},{9,15},{10,... | collective-permute-start | bytes 18008 | tf_op jit(solution)/shard_map/ppermute | solution.py:282
  9.2 6.4 %collective-permute-start.6 = (bf16[2,1500]{1,0:T(2,128)(2,1)}, bf16[2,1500]{1,0:T(2,128)(2,1)S(1)}, u32[]{:S(2)}, u32[]{:S(2)}) collective-permute-start(bf16[2,1500]{1,0:T(2,128)(2,1)} %get-tuple-element.72), channel_id=1, source_target_pairs={{0,7},{1,6},{2,5},{3,4},{4,3},{5,2},{6,1},{7,0},{8,15},{9,14},{10,... | collective-permute-start | bytes 18008 | tf_op jit(solution)/shard_map/ppermute | solution.py:282
  9.3 9.9 %collective-permute-start.7 = (bf16[2,1500]{1,0:T(2,128)(2,1)}, bf16[2,1500]{1,0:T(2,128)(2,1)S(1)}, u32[]{:S(2)}, u32[]{:S(2)}) collective-permute-start(bf16[2,1500]{1,0:T(2,128)(2,1)} %get-tuple-element.73), channel_id=1, source_target_pairs={{0,8},{1,9},{2,10},{3,11},{4,12},{5,13},{6,14},{7,15},{8,0},{9,1},... | collective-permute-start | bytes 18008 | tf_op jit(solution)/shard_map/ppermute | solution.py:282
  12.0 7.3 %collective-permute-start.8 = (bf16[2,1500]{1,0:T(2,128)(2,1)}, bf16[2,1500]{1,0:T(2,128)(2,1)S(1)}, u32[]{:S(2)}, u32[]{:S(2)}) collective-permute-start(bf16[2,1500]{1,0:T(2,128)(2,1)} %get-tuple-element.74), channel_id=1, source_target_pairs={{0,9},{1,8},{2,11},{3,10},{4,13},{5,12},{6,15},{7,14},{8,1},{9,0},... | collective-permute-start | bytes 18008 | tf_op jit(solution)/shard_map/ppermute | solution.py:282
  12.0 11.6 %collective-permute-start.9 = (bf16[2,1500]{1,0:T(2,128)(2,1)}, bf16[2,1500]{1,0:T(2,128)(2,1)S(1)}, u32[]{:S(2)}, u32[]{:S(2)}) collective-permute-start(bf16[2,1500]{1,0:T(2,128)(2,1)} %get-tuple-element.75), channel_id=1, source_target_pairs={{0,10},{1,11},{2,8},{3,9},{4,14},{5,15},{6,12},{7,13},{8,2},{9,3},... | collective-permute-start | bytes 18008 | tf_op jit(solution)/shard_map/ppermute | solution.py:282
  15.5 12.0 %collective-permute-start.10 = (bf16[2,1500]{1,0:T(2,128)(2,1)}, bf16[2,1500]{1,0:T(2,128)(2,1)S(1)}, u32[]{:S(2)}, u32[]{:S(2)}) collective-permute-start(bf16[2,1500]{1,0:T(2,128)(2,1)} %get-tuple-element.76), channel_id=1, source_target_pairs={{0,11},{1,10},{2,9},{3,8},{4,15},{5,14},{6,13},{7,12},{8,3},{9,2},... | collective-permute-start | bytes 18008 | tf_op jit(solution)/shard_map/ppermute | solution.py:282
  15.7 11.9 %collective-permute-start.11 = (bf16[2,1500]{1,0:T(2,128)(2,1)}, bf16[2,1500]{1,0:T(2,128)(2,1)S(1)}, u32[]{:S(2)}, u32[]{:S(2)}) collective-permute-start(bf16[2,1500]{1,0:T(2,128)(2,1)} %get-tuple-element.77), channel_id=1, source_target_pairs={{0,12},{1,13},{2,14},{3,15},{4,8},{5,9},{6,10},{7,11},{8,4},{9,5},... | collective-permute-start | bytes 18008 | tf_op jit(solution)/shard_map/ppermute | solution.py:282
  19.2 8.4 %collective-permute-start.12 = (bf16[2,1500]{1,0:T(2,128)(2,1)}, bf16[2,1500]{1,0:T(2,128)(2,1)S(1)}, u32[]{:S(2)}, u32[]{:S(2)}) collective-permute-start(bf16[2,1500]{1,0:T(2,128)(2,1)} %get-tuple-element.78), channel_id=1, source_target_pairs={{0,13},{1,12},{2,15},{3,14},{4,9},{5,8},{6,11},{7,10},{8,5},{9,4},... | collective-permute-start | bytes 18008 | tf_op jit(solution)/shard_map/ppermute | solution.py:282
  19.2 8.3 %collective-permute-start.13 = (bf16[2,1500]{1,0:T(2,128)(2,1)}, bf16[2,1500]{1,0:T(2,128)(2,1)S(1)}, u32[]{:S(2)}, u32[]{:S(2)}) collective-permute-start(bf16[2,1500]{1,0:T(2,128)(2,1)} %get-tuple-element.79), channel_id=1, source_target_pairs={{0,14},{1,15},{2,12},{3,13},{4,10},{5,11},{6,8},{7,9},{8,6},{9,7},... | collective-permute-start | bytes 18008 | tf_op jit(solution)/shard_map/ppermute | solution.py:282
  23.7 6.0 %collective-permute-start.14 = (bf16[2,1500]{1,0:T(2,128)(2,1)}, bf16[2,1500]{1,0:T(2,128)(2,1)S(1)}, u32[]{:S(2)}, u32[]{:S(2)}) collective-permute-start(bf16[2,1500]{1,0:T(2,128)(2,1)} %get-tuple-element.80), channel_id=1, source_target_pairs={{0,15},{1,14},{2,13},{3,12},{4,11},{5,10},{6,9},{7,8},{8,7},{9,6},... | collective-permute-start | bytes 18008 | tf_op jit(solution)/shard_map/ppermute | solution.py:282
  39.4 5.6 %collective-permute-start.17 = (bf16[2,1500]{1,0:T(2,128)(2,1)S(1)}, bf16[2,1500]{1,0:T(2,128)(2,1)S(1)}, u32[]{:S(2)}, u32[]{:S(2)}) collective-permute-start(bf16[2,1500]{1,0:T(2,128)(2,1)S(1)} %get-tuple-element.84), channel_id=1, source_target_pairs={{0,3},{1,2},{2,1},{3,0},{4,7},{5,6},{6,5},{7,4},{8,11},{9,10},{10,... | collective-permute-start | bytes 18008 | tf_op jit(solution)/shard_map/ppermute | solution.py:282
  40.6 7.1 %collective-permute-start.19 = (bf16[2,1500]{1,0:T(2,128)(2,1)S(1)}, bf16[2,1500]{1,0:T(2,128)(2,1)S(1)}, u32[]{:S(2)}, u32[]{:S(2)}) collective-permute-start(bf16[2,1500]{1,0:T(2,128)(2,1)S(1)} %get-tuple-element.86), channel_id=1, source_target_pairs={{0,5},{1,4},{2,7},{3,6},{4,1},{5,0},{6,3},{7,2},{8,13},{9,12},{10,... | collective-permute-start | bytes 18008 | tf_op jit(solution)/shard_map/ppermute | solution.py:282
  42.4 6.7 %collective-permute-start.20 = (bf16[2,1500]{1,0:T(2,128)(2,1)S(1)}, bf16[2,1500]{1,0:T(2,128)(2,1)S(1)}, u32[]{:S(2)}, u32[]{:S(2)}) collective-permute-start(bf16[2,1500]{1,0:T(2,128)(2,1)S(1)} %get-tuple-element.87), channel_id=1, source_target_pairs={{0,6},{1,7},{2,4},{3,5},{4,2},{5,3},{6,0},{7,1},{8,14},{9,15},{10,... | collective-permute-start | bytes 18008 | tf_op jit(solution)/shard_map/ppermute | solution.py:282
  42.6 8.6 %collective-permute-start.21 = (bf16[2,1500]{1,0:T(2,128)(2,1)S(1)}, bf16[2,1500]{1,0:T(2,128)(2,1)S(1)}, u32[]{:S(2)}, u32[]{:S(2)}) collective-permute-start(bf16[2,1500]{1,0:T(2,128)(2,1)S(1)} %get-tuple-element.88), channel_id=1, source_target_pairs={{0,7},{1,6},{2,5},{3,4},{4,3},{5,2},{6,1},{7,0},{8,15},{9,14},{10,... | collective-permute-start | bytes 18008 | tf_op jit(solution)/shard_map/ppermute | solution.py:282
  45.0 7.7 %collective-permute-start.22 = (bf16[2,1500]{1,0:T(2,128)(2,1)S(1)}, bf16[2,1500]{1,0:T(2,128)(2,1)S(1)}, u32[]{:S(2)}, u32[]{:S(2)}) collective-permute-start(bf16[2,1500]{1,0:T(2,128)(2,1)S(1)} %get-tuple-element.89), channel_id=1, source_target_pairs={{0,8},{1,9},{2,10},{3,11},{4,12},{5,13},{6,14},{7,15},{8,0},{9,1},... | collective-permute-start | bytes 18008 | tf_op jit(solution)/shard_map/ppermute | solution.py:282
  45.6 9.2 %collective-permute-start.23 = (bf16[2,1500]{1,0:T(2,128)(2,1)S(1)}, bf16[2,1500]{1,0:T(2,128)(2,1)S(1)}, u32[]{:S(2)}, u32[]{:S(2)}) collective-permute-start(bf16[2,1500]{1,0:T(2,128)(2,1)S(1)} %get-tuple-element.90), channel_id=1, source_target_pairs={{0,9},{1,8},{2,11},{3,10},{4,13},{5,12},{6,15},{7,14},{8,1},{9,0},... | collective-permute-start | bytes 18008 | tf_op jit(solution)/shard_map/ppermute | solution.py:282
  47.7 9.6 %collective-permute-start.24 = (bf16[2,1500]{1,0:T(2,128)(2,1)S(1)}, bf16[2,1500]{1,0:T(2,128)(2,1)S(1)}, u32[]{:S(2)}, u32[]{:S(2)}) collective-permute-start(bf16[2,1500]{1,0:T(2,128)(2,1)S(1)} %get-tuple-element.91), channel_id=1, source_target_pairs={{0,10},{1,11},{2,8},{3,9},{4,14},{5,15},{6,12},{7,13},{8,2},{9,3},... | collective-permute-start | bytes 18008 | tf_op jit(solution)/shard_map/ppermute | solution.py:282
  49.1 10.1 %collective-permute-start.25 = (bf16[2,1500]{1,0:T(2,128)(2,1)S(1)}, bf16[2,1500]{1,0:T(2,128)(2,1)S(1)}, u32[]{:S(2)}, u32[]{:S(2)}) collective-permute-start(bf16[2,1500]{1,0:T(2,128)(2,1)S(1)} %get-tuple-element.92), channel_id=1, source_target_pairs={{0,11},{1,10},{2,9},{3,8},{4,15},{5,14},{6,13},{7,12},{8,3},{9,2},... | collective-permute-start | bytes 18008 | tf_op jit(solution)/shard_map/ppermute | solution.py:282
  51.2 8.0 %collective-permute-start.26 = (bf16[2,1500]{1,0:T(2,128)(2,1)S(1)}, bf16[2,1500]{1,0:T(2,128)(2,1)S(1)}, u32[]{:S(2)}, u32[]{:S(2)}) collective-permute-start(bf16[2,1500]{1,0:T(2,128)(2,1)S(1)} %get-tuple-element.93), channel_id=1, source_target_pairs={{0,12},{1,13},{2,14},{3,15},{4,8},{5,9},{6,10},{7,11},{8,4},{9,5},... | collective-permute-start | bytes 18008 | tf_op jit(solution)/shard_map/ppermute | solution.py:282
  52.6 6.6 %collective-permute-start.27 = (bf16[2,1500]{1,0:T(2,128)(2,1)S(1)}, bf16[2,1500]{1,0:T(2,128)(2,1)S(1)}, u32[]{:S(2)}, u32[]{:S(2)}) collective-permute-start(bf16[2,1500]{1,0:T(2,128)(2,1)S(1)} %get-tuple-element.94), channel_id=1, source_target_pairs={{0,13},{1,12},{2,15},{3,14},{4,9},{5,8},{6,11},{7,10},{8,5},{9,4},... | collective-permute-start | bytes 18008 | tf_op jit(solution)/shard_map/ppermute | solution.py:282
  54.8 6.3 %collective-permute-start.28 = (bf16[2,1500]{1,0:T(2,128)(2,1)S(1)}, bf16[2,1500]{1,0:T(2,128)(2,1)S(1)}, u32[]{:S(2)}, u32[]{:S(2)}) collective-permute-start(bf16[2,1500]{1,0:T(2,128)(2,1)S(1)} %get-tuple-element.95), channel_id=1, source_target_pairs={{0,14},{1,15},{2,12},{3,13},{4,10},{5,11},{6,8},{7,9},{8,6},{9,7},... | collective-permute-start | bytes 18008 | tf_op jit(solution)/shard_map/ppermute | solution.py:282
  57.3 5.8 %collective-permute-start.29 = (bf16[2,1500]{1,0:T(2,128)(2,1)S(1)}, bf16[2,1500]{1,0:T(2,128)(2,1)S(1)}, u32[]{:S(2)}, u32[]{:S(2)}) collective-permute-start(bf16[2,1500]{1,0:T(2,128)(2,1)S(1)} %get-tuple-element.96), channel_id=1, source_target_pairs={{0,15},{1,14},{2,13},{3,12},{4,11},{5,10},{6,9},{7,8},{8,7},{9,6},... | collective-permute-start | bytes 18008 | tf_op jit(solution)/shard_map/ppermute | solution.py:282
  (25 other events, 203.2 us)
